TPU v7x, 32 devices: a whole 2x2x4 slice. The times are simulated.
32 devices in a mesh: facet: 4 (over x, core), sub: 4 (over z), wa: 2 (over y).
Axes of the slice: x: 2, y: 2, z: 4, core: 2. Of those that a mesh axis runs over, the one named last changes fastest.
Arguments:
- facets: float32 [4, 128, 2, 4096], P('facet'), may hold values from -6 to 6
- correction: float32 [4, 4096], P('facet'), may hold values from 0.5 to 2
- window: float32 [128], replicated, may hold values from 0.25 to 1
- offsets: int32 [8], replicated, may hold values from 0 to 4095
- phases: float32 [4, 512], P('wa'), may hold values from -3.140625 to 3.140625
- coverage: int32 [8, 4, 512], P('sub', 'wa'), may hold values from 0 to 3
Outputs:
- facets_out: float32 [4, 128, 2, 4096], P('facet', ('sub', 'wa'))
All inputs are finite; a program needn't handle non-finite values.
Results may differ from a plain program's by a relative error of at most 0.0001.
Values sent between devices are 32-bit elements; how exact they have to be, the bound alone decides.
A program may use at most 192 MiB of HBM per device.

v0:
```python
import math

import jax
import jax.numpy as jnp
from jax import lax
from jax.sharding import PartitionSpec as P

WPLANES = 4


exact_mode = lax.Precision.HIGHEST


def angles(left_idx, right_idx, length):
    product = left_idx[:, None] * right_idx[None, :] % length
    radians = product.astype(jnp.float32) * (2.0 * math.pi / length)
    return (jnp.cos(radians), jnp.sin(radians))


def split_factor(length):
    factor = 1
    for cand in range(1, length + 1):
        if length % cand == 0 and cand * cand <= length:
            factor = cand
    return factor


def factored_transform(real_in, imag_in, sign):
    length = real_in.shape[-1]
    first = split_factor(length)
    second = length // first
    leading = real_in.shape[:-1]
    real_x = real_in.reshape(leading + (first, second))
    imag_x = imag_in.reshape(leading + (first, second))
    first_index = jnp.arange(first, dtype=jnp.int32)
    second_index = jnp.arange(second, dtype=jnp.int32)
    cos_a, sin_a = angles(first_index, first_index, first)
    sin_a = sin_a * sign
    real_y = jnp.einsum("...ab,ak->...kb", real_x, cos_a, precision=exact_mode) - jnp.einsum(
        "...ab,ak->...kb", imag_x, sin_a, precision=exact_mode
    )
    imag_y = jnp.einsum("...ab,ak->...kb", real_x, sin_a, precision=exact_mode) + jnp.einsum(
        "...ab,ak->...kb", imag_x, cos_a, precision=exact_mode
    )
    twist_cos, twist_sin = angles(first_index, second_index, length)
    twist_sin = twist_sin * sign
    real_t = real_y * twist_cos - imag_y * twist_sin
    imag_t = real_y * twist_sin + imag_y * twist_cos
    cos_b, sin_b = angles(second_index, second_index, second)
    sin_b = sin_b * sign
    real_z = jnp.einsum("...kb,bm->...mk", real_t, cos_b, precision=exact_mode) - jnp.einsum(
        "...kb,bm->...mk", imag_t, sin_b, precision=exact_mode
    )
    imag_z = jnp.einsum("...kb,bm->...mk", real_t, sin_b, precision=exact_mode) + jnp.einsum(
        "...kb,bm->...mk", imag_t, cos_b, precision=exact_mode
    )
    scale = length ** (-0.5)
    return (
        real_z.reshape(leading + (length,)) * scale,
        imag_z.reshape(leading + (length,)) * scale,
    )


def facet_blocks(facets, correction, window, offsets_here):
    block_width = window.shape[0]
    block_index = jnp.arange(block_width, dtype=jnp.int32)
    scaled = facets[0] * correction[0][None, None, :]
    real_spec, imag_spec = factored_transform(scaled[:, 0], scaled[:, 1], -1.0)
    spectrum = jnp.stack([real_spec, imag_spec], axis=1)
    doubled = jnp.concatenate([spectrum, spectrum], axis=2)

    def cut_block(offset_one):
        return lax.dynamic_slice_in_dim(doubled, offset_one, block_width, 2)

    cut = jax.vmap(cut_block)(offsets_here)
    real_seg = jnp.transpose(cut[:, :, 0], (1, 0, 2)) * window
    imag_seg = jnp.transpose(cut[:, :, 1], (1, 0, 2)) * window
    row_count = real_seg.shape[0]
    subgrid_count = real_seg.shape[1]
    small_cos, small_sin = angles(block_index, block_index, block_width)
    small_table = jnp.concatenate([small_cos, small_sin], axis=1) * block_width ** (-0.5)
    stacked = jnp.stack([real_seg, imag_seg], axis=2)
    mixed_rows = jnp.dot(stacked.reshape(-1, block_width), small_table, precision=exact_mode)
    mixed_rows = mixed_rows.reshape(row_count, subgrid_count, 2, 2, block_width)
    real_part = mixed_rows[:, :, 0, 0] - mixed_rows[:, :, 1, 1]
    imag_part = mixed_rows[:, :, 0, 1] + mixed_rows[:, :, 1, 0]
    return jnp.stack([real_part, imag_part], axis=2)


def along_outer(values, matrix):
    return jnp.einsum("wqajm,ak->wqkjm", values, matrix, precision=exact_mode)


def along_inner(values, matrix):
    return jnp.einsum("wqkjm,mn->wqkjn", values, matrix, precision=exact_mode)


def subgrid_adjoint(blocks, phases, coverage):
    facet_count = blocks.shape[1]
    block_width = blocks.shape[4]
    length = facet_count * block_width
    local_planes = phases.shape[0]
    real_in = blocks[:, :, :, 0]
    imag_in = blocks[:, :, :, 1]
    screen = phases.reshape(local_planes, 1, facet_count, 1, block_width)
    kernel_cos = jnp.cos(screen)
    kernel_sin = jnp.sin(screen)
    real_z = real_in[None] * kernel_cos - imag_in[None] * kernel_sin
    imag_z = real_in[None] * kernel_sin + imag_in[None] * kernel_cos
    outer_index = jnp.arange(facet_count, dtype=jnp.int32)
    inner_index = jnp.arange(block_width, dtype=jnp.int32)
    outer_cos, outer_sin = angles(outer_index, outer_index, facet_count)
    inner_cos, inner_sin = angles(inner_index, inner_index, block_width)
    turn_cos, turn_sin = angles(outer_index, inner_index, length)
    turn_cos = turn_cos[None, None, :, None, :]
    turn_sin = turn_sin[None, None, :, None, :]
    real_a = along_outer(real_z, outer_cos) + along_outer(imag_z, outer_sin)
    imag_a = along_outer(imag_z, outer_cos) - along_outer(real_z, outer_sin)
    real_b = real_a * turn_cos + imag_a * turn_sin
    imag_b = imag_a * turn_cos - real_a * turn_sin
    real_g = along_inner(real_b, inner_cos) + along_inner(imag_b, inner_sin)
    imag_g = along_inner(imag_b, inner_cos) - along_inner(real_b, inner_sin)
    counts = coverage.reshape(coverage.shape[0], local_planes, block_width, facet_count)
    counts = jnp.transpose(counts, (1, 3, 0, 2))[:, None]
    real_v = real_g * counts
    imag_v = imag_g * counts
    real_p = along_inner(real_v, inner_cos) - along_inner(imag_v, inner_sin)
    imag_p = along_inner(real_v, inner_sin) + along_inner(imag_v, inner_cos)
    real_q = real_p * turn_cos - imag_p * turn_sin
    imag_q = real_p * turn_sin + imag_p * turn_cos
    real_y = jnp.einsum("wqkjm,ka->wqajm", real_q, outer_cos, precision=exact_mode) - jnp.einsum(
        "wqkjm,ka->wqajm", imag_q, outer_sin, precision=exact_mode
    )
    imag_y = jnp.einsum("wqkjm,ka->wqajm", real_q, outer_sin, precision=exact_mode) + jnp.einsum(
        "wqkjm,ka->wqajm", imag_q, outer_cos, precision=exact_mode
    )
    factor = 1.0 / (length * WPLANES)
    real_h = jnp.sum(real_y * kernel_cos + imag_y * kernel_sin, axis=0) * factor
    imag_h = jnp.sum(imag_y * kernel_cos - real_y * kernel_sin, axis=0) * factor
    return jnp.stack([real_h, imag_h], axis=3)


def facet_image(segments, offsets_here, window, correction):
    row_count = segments.shape[0]
    block_width = segments.shape[3]
    length = correction.shape[1]
    block_index = jnp.arange(block_width, dtype=jnp.int32)
    small_cos, small_sin = angles(block_index, block_index, block_width)
    small_table = jnp.concatenate([small_cos, small_sin], axis=1) * block_width ** (-0.5)
    mixed_rows = jnp.dot(segments.reshape(-1, block_width), small_table, precision=exact_mode)
    mixed_rows = mixed_rows.reshape(row_count, segments.shape[1], 2, 2, block_width)
    real_seg = (mixed_rows[:, :, 0, 0] + mixed_rows[:, :, 1, 1]) * window
    imag_seg = (mixed_rows[:, :, 1, 0] - mixed_rows[:, :, 0, 1]) * window
    joined = jnp.transpose(jnp.stack([real_seg, imag_seg], axis=2), (1, 0, 2, 3))

    def add_subgrid(running, inputs):
        seg_rows, offset_one = inputs
        current = lax.dynamic_slice_in_dim(running, offset_one, block_width, 2)
        return (lax.dynamic_update_slice_in_dim(running, current + seg_rows, offset_one, 2), None)

    initial = jnp.zeros((row_count, 2, 2 * length), jnp.float32)
    doubled, unused = lax.scan(add_subgrid, initial, (joined, offsets_here))
    folded = doubled[:, :, :length] + doubled[:, :, length:]
    real_out, imag_out = factored_transform(folded[:, 0], folded[:, 1], 1.0)
    return jnp.stack([real_out, imag_out], axis=1) * correction[0]


def on_device(facets, correction, window, offsets, phases, coverage):
    sub_count = lax.axis_size("sub")
    pair_count = lax.axis_size("wa")
    facet_count = lax.axis_size("facet")
    sub_index = lax.axis_index("sub")
    pair_index = lax.axis_index("wa")
    per_owner = coverage.shape[0]
    row_dev = facets.shape[1] // facet_count
    block_width = window.shape[0]
    eighth = row_dev // (sub_count * pair_count)
    owner_offsets = lax.dynamic_slice_in_dim(offsets, sub_index * per_owner, per_owner)
    all_phases, all_counts = (
        lax.all_gather(phases, "wa", axis=0, tiled=True),
        lax.all_gather(coverage.astype(jnp.float32), "wa", axis=1, tiled=True),
    )
    length = facets.shape[3]
    grouped = facets.reshape(1, sub_count, pair_count, eighth * facet_count, 2, length)
    mine = lax.dynamic_index_in_dim(grouped, pair_index, 2, keepdims=False)
    mine = mine.reshape(1, sub_count * eighth * facet_count, 2, length)
    blocks = facet_blocks(mine, correction, window, owner_offsets)
    blocks = blocks.reshape(sub_count * eighth, facet_count, per_owner, 2, block_width)
    partial_value = subgrid_adjoint(
        lax.all_to_all(blocks, "facet", split_axis=1, concat_axis=1, tiled=True),
        all_phases,
        all_counts,
    )
    summed = partial_value.reshape(sub_count, eighth, facet_count, per_owner, 2, block_width)
    returned = lax.all_to_all(summed, "facet", split_axis=2, concat_axis=2, tiled=True)
    regrouped = lax.all_to_all(returned, "sub", split_axis=0, concat_axis=3, tiled=True)
    regrouped = regrouped.reshape(eighth * facet_count, per_owner * sub_count, 2, block_width)
    facet_out = facet_image(regrouped, offsets, window, correction)
    return facet_out.reshape(1, eighth * facet_count, 2, facet_out.shape[-1])


def solution(mesh):
    return jax.shard_map(
        on_device,
        mesh=mesh,
        in_specs=(
            P("facet", None, None, None),
            P("facet", None),
            P(),
            P(),
            P("wa", None),
            P("sub", "wa", None),
        ),
        out_specs=P("facet", ("sub", "wa"), None, None),
        check_vma=False,
    )
```

profile of v0, /device:TPU:0, one launch (start us, length us, event | category | flops | bytes accessed | tf_op | source)
XLA Modules:
  0.0 203.4 jit_solution(9885606678406070389)
XLA Ops:
  0.0 1.7 constant_dynamic-slice_fusion.1
  1.7 1.2 copy.98
  3.2 1.1 fusion.314
  4.3 2.2 %reshape_squeeze.12 = f32[64,64,64]{2,1,0:T(8,128)S(1)} reshape(f32[64,1,4096]{2,0,1:T(8,128)} %get-tuple-element.57) | data formatting | bytes 2097152 | tf_op jit(solution)/shard_map/reshape;squeeze | solution.py:33
  6.5 3.4 %fusion.106 = f32[64,64,64]{2,0,1:T(8,128)} fusion(f32[64,64,64]{2,1,0:T(8,128)S(1)} %reshape_squeeze.12), kind=kOutput, calls=%fused_computation.163 | convolution fusion | flops 201383936 | bytes 2097152 | tf_op jit(solution)/shard_map/...ab,ak->...kb/dot_general | solution.py:39
  9.9 3.4 %fusion.95 = f32[64,64,64]{2,0,1:T(8,128)} fusion(f32[64,64,64]{2,1,0:T(8,128)S(1)} %reshape_squeeze.12), kind=kOutput, calls=%fused_computation.152 | convolution fusion | flops 201388032 | bytes 2097152 | tf_op jit(solution)/shard_map/...ab,ak->...kb/dot_general | solution.py:42
  13.6 2.2 %reshape_squeeze.13 = f32[64,64,64]{2,1,0:T(8,128)} reshape(f32[64,1,4096]{2,0,1:T(8,128)S(1)} %get-tuple-element.56) | data formatting | bytes 2097152 | tf_op jit(solution)/shard_map/reshape;squeeze | solution.py:34
  15.8 4.4 %convolution_subtract_fusion = f32[64,64,64]{2,0,1:T(8,128)S(1)} fusion(f32[64,64,64]{2,0,1:T(8,128)} %fusion.106, f32[64,64,64]{2,1,0:T(8,128)} %reshape_squeeze.13), kind=kOutput, calls=%fused_computation.18 | convolution fusion | flops 201650176 | bytes 3145728 | tf_op jit(solution)/shard_map/...ab,ak->...kb/dot_general | solution.py:39
  20.2 3.5 %convolution_add_fusion = f32[64,64,64]{2,0,1:T(8,128)} fusion(f32[64,64,64]{2,0,1:T(8,128)S(1)} %copy-done.2, f32[64,64,64]{2,1,0:T(8,128)S(1)} %copy-done.1), kind=kOutput, calls=%fused_computation.17 | convolution fusion | flops 201646080 | bytes 3145728 | tf_op jit(solution)/shard_map/...ab,ak->...kb/dot_general | solution.py:42
  23.9 9.4 %fusion.3 = f32[64,64,64]{2,0,1:T(8,128)} fusion(f32[64,64,64]{2,0,1:T(8,128)} %convolution_add_fusion, f32[64,64,64]{2,0,1:T(8,128)S(1)} %convolution_subtract_fusion, f32[64,64]{1,0:T(8,128)S(1)} %copy.100, f32[64,64]{1,0:T(8,128)S(1)} %copy.99), kind=kOutput, calls=%fused_computation.7 | convolution fusion | flops 202174464 | bytes 3178496 | tf_op jit(solution)/shard_map/...kb,bm->...mk/dot_general | solution.py:51
  33.3 7.6 %fusion.1 = f32[64,64,64]{2,0,1:T(8,128)} fusion(f32[64,64,64]{2,0,1:T(8,128)S(1)} %copy-done, f32[64,64,64]{2,0,1:T(8,128)S(1)} %convolution_subtract_fusion, f32[64,64]{1,0:T(8,128)S(1)} %copy.100, f32[64,64]{1,0:T(8,128)S(1)} %copy.99), kind=kOutput, calls=%fused_computation.5 | convolution fusion | flops 202170368 | bytes 3178496 | tf_op jit(solution)/shard_map/...kb,bm->...mk/dot_general | solution.py:54
  41.2 9.7 %multiply_bitcast_fusion.1 = f32[64,64,64]{2,1,0:T(8,128)} fusion(f32[64,64,64]{2,0,1:T(8,128)} %fusion.3, f32[64,64,64]{2,0,1:T(8,128)} %convolution_add_fusion, f32[64,64,64]{2,0,1:T(8,128)S(1)} %convolution_subtract_fusion, f32[64,64]{1,0:T(8,128)S(1)} %copy.100, f32[64,64]{1,0:T(8,128)S(1)} %copy.99), kind=kOutput, calls=%fused_computation.14 | convolution fusion | flops 202694656 | bytes 4227072 | tf_op jit(solution)/shard_map/...kb,bm->...mk/dot_general | solution.py:51
  50.9 3.7 %copy.141 = f32[64,64,64]{0,2,1:T(8,128)} copy(f32[64,64,64]{2,1,0:T(8,128)} %multiply_bitcast_fusion.1) | data formatting | bytes 2097152 | tf_op jit(solution)/shard_map/mul | solution.py:59
  54.7 9.7 %multiply_bitcast_fusion = f32[64,64,64]{2,1,0:T(8,128)} fusion(f32[64,64,64]{2,0,1:T(8,128)} %fusion.1, f32[64,64,64]{2,0,1:T(8,128)} %convolution_add_fusion, f32[64,64,64]{2,0,1:T(8,128)S(1)} %convolution_subtract_fusion, f32[64,64]{1,0:T(8,128)S(1)} %copy.100, f32[64,64]{1,0:T(8,128)S(1)} %copy.99), kind=kOutput, calls=%fused_computation.13 | convolution fusion | flops 202698752 | bytes 4227072 | tf_op jit(solution)/shard_map/...kb,bm->...mk/dot_general | solution.py:54
  64.4 3.5 %copy.142 = f32[64,64,64]{0,2,1:T(8,128)} copy(f32[64,64,64]{2,1,0:T(8,128)} %multiply_bitcast_fusion) | data formatting | bytes 2097152 | tf_op jit(solution)/shard_map/mul | solution.py:60
  67.9 30.4 %maximum_maximum_fusion = f32[64,2,8192]{0,1,2:T(2,128)} fusion(f32[64,1,4096]{0,1,2:T(1,128)} %bitcast.230, f32[64,1,4096]{0,1,2:T(1,128)S(1)} %bitcast.229), kind=kLoop, calls=%fused_computation.4 | loop fusion | flops 3145728 | bytes 6291456 | tf_op jit(solution)/shard_map/concatenate | solution.py:70
  98.4 4.2 %gather_fusion = f32[2,64,2,128]{1,2,3,0:T(2,128)S(1)} fusion(f32[64,2,8192]{0,1,2:T(2,128)} %maximum_maximum_fusion, s32[2]{0:T(128)S(1)} %fusion.180), kind=kCustom, calls=%fused_computation | custom fusion | bytes 262168 | tf_op jit(solution)/shard_map/vmap()/gather | solution.py:73
  103.6 0.7 pad_maximum_fusion
  104.2 4.2 %all-to-all-start = ((f32[16,4,2,2,128]{4,0,2,3,1:T(8,128)}), f32[16,4,2,2,128]{4,0,2,3,1:T(8,128)S(1)}, u32[]{:S(2)}, u32[]{:S(2)}) async-start(f32[16,4,2,2,128]{4,0,2,3,1:T(8,128)} %pad_maximum_fusion), calls=%async_computation | async-start | bytes 262144 | tf_op jit(solution)/shard_map/all_to_all | solution.py:190
  108.4 4.4 %all-gather = f32[2,2,512]{2,1,0:T(2,128)S(1)} all-gather(f32[1,2,512]{2,1,0:T(2,128)S(1)} %bitcast.243), channel_id=1, replica_groups=mesh['facet'=4,'sub'=4,'wa'=2] {'wa'}, dimensions={0}, use_global_device_ids=true | all-gather | bytes 12288 | tf_op jit(solution)/shard_map/all_gather | solution.py:180
  113.0 4.5 %all_gather.7 = f32[2,4,512]{2,0,1:T(2,128)S(1)} all-gather(f32[2,2,512]{2,0,1:T(2,128)S(1)} %copy_convert_fusion), channel_id=1, replica_groups=mesh['facet'=4,'sub'=4,'wa'=2] {'wa'}, dimensions={1}, use_global_device_ids=true | all-gather | bytes 24576 | tf_op jit(solution)/shard_map/all_gather | solution.py:181
  120.3 0.7 subtract_bitcast_fusion
  126.0 0.7 fusion.39
  126.7 0.7 fusion.37
  127.4 0.7 fusion.20
  128.2 0.9 add_reduce_fusion
  129.1 7.7 %all_to_all.25 = f32[4,4,4,2,2,128]{5,1,0,3,4,2:T(4,128)S(1)} all-to-all(f32[4,4,4,2,2,128]{5,1,0,3,4,2:T(4,128)S(1)} %copy.124), channel_id=1, replica_groups=mesh['facet'=4,'sub'=4,'wa'=2] {'facet'}, dimensions={2} | all-to-all | bytes 262144 | tf_op jit(solution)/shard_map/all_to_all | solution.py:195
  136.9 0.7 copy.125
  137.5 5.6 %all-to-all-start.2 = ((f32[4,4,4,2,2,128]{5,1,3,2,4,0:T(4,128)}), f32[4,4,4,2,2,128]{5,1,3,2,4,0:T(4,128)S(1)}, u32[]{:S(2)}, u32[]{:S(2)}) async-start(f32[4,4,4,2,2,128]{5,1,3,2,4,0:T(4,128)} %copy.125), calls=%async_computation.2 | async-start | bytes 262144 | tf_op jit(solution)/shard_map/all_to_all | solution.py:196
  143.3 5.7 %all-to-all-done.2 = f32[4,4,4,2,2,128]{5,1,3,2,4,0:T(4,128)S(1)} async-done(((f32[4,4,4,2,2,128]{5,1,3,2,4,0:T(4,128)}), f32[4,4,4,2,2,128]{5,1,3,2,4,0:T(4,128)S(1)}, u32[]{:S(2)}, u32[]{:S(2)}) %all-to-all-start.2) | async-done | bytes 131104 | tf_op jit(solution)/shard_map/all_to_all | solution.py:196
  149.9 39.4 %while.10 = (s32[]{:T(128)}, f32[16,2,8192]{2,1,0:T(2,128)S(1)}, s32[8]{0:T(128)S(1)}, f32[8,16,2,128]{3,0,1,2:T(8,128)S(1)}, s32[]{:T(128)}, /*index=5*/s32[]{:T(128)}, s32[]{:T(128)}) while((s32[]{:T(128)}, f32[16,2,8192]{2,1,0:T(2,128)S(1)}, s32[8]{0:T(128)S(1)}, f32[8,16,2,128]{3,0,1,2:T(8,128)S(1)}, s32[]{:T(128)}, /*index=5*/s32[]{:T(128)}, ...), condition=%wide.region_3.4_spmd, body=%wide.region_2.3_spmd.sunk | while | flops 4101 | bytes 114823 | solution.py:162
  152.6 2.5 %dynamic_update_slice.4 = f32[16,2,8192]{2,1,0:T(2,128)S(1)} dynamic-update-slice(f32[16,2,8192]{2,1,0:T(2,128)S(1)} %get-tuple-element.111, f32[16,2,128]{2,1,0:T(2,128)S(1)} %fusion.336, s32[]{:T(128)} %constant.113.clone.1..sunk, s32[]{:T(128)} %constant.113.clone.1..sunk, s32[]{:T(128)S(6)} %select_n.325) | dynamic-update-slice | bytes 32772 | tf_op jit(solution)/shard_map/while/body/eval_jaxpr/dynamic_update_slice | solution.py:159
  157.8 2.5 %dynamic_update_slice.4 = f32[16,2,8192]{2,1,0:T(2,128)S(1)} dynamic-update-slice(f32[16,2,8192]{2,1,0:T(2,128)S(1)} %get-tuple-element.111, f32[16,2,128]{2,1,0:T(2,128)S(1)} %fusion.336, s32[]{:T(128)} %constant.113.clone.1..sunk, s32[]{:T(128)} %constant.113.clone.1..sunk, s32[]{:T(128)S(6)} %select_n.325) | dynamic-update-slice | bytes 32772 | tf_op jit(solution)/shard_map/while/body/eval_jaxpr/dynamic_update_slice | solution.py:159
  163.0 2.5 %dynamic_update_slice.4 = f32[16,2,8192]{2,1,0:T(2,128)S(1)} dynamic-update-slice(f32[16,2,8192]{2,1,0:T(2,128)S(1)} %get-tuple-element.111, f32[16,2,128]{2,1,0:T(2,128)S(1)} %fusion.336, s32[]{:T(128)} %constant.113.clone.1..sunk, s32[]{:T(128)} %constant.113.clone.1..sunk, s32[]{:T(128)S(6)} %select_n.325) | dynamic-update-slice | bytes 32772 | tf_op jit(solution)/shard_map/while/body/eval_jaxpr/dynamic_update_slice | solution.py:159
  168.2 2.5 %dynamic_update_slice.4 = f32[16,2,8192]{2,1,0:T(2,128)S(1)} dynamic-update-slice(f32[16,2,8192]{2,1,0:T(2,128)S(1)} %get-tuple-element.111, f32[16,2,128]{2,1,0:T(2,128)S(1)} %fusion.336, s32[]{:T(128)} %constant.113.clone.1..sunk, s32[]{:T(128)} %constant.113.clone.1..sunk, s32[]{:T(128)S(6)} %select_n.325) | dynamic-update-slice | bytes 32772 | tf_op jit(solution)/shard_map/while/body/eval_jaxpr/dynamic_update_slice | solution.py:159
  173.4 2.5 %dynamic_update_slice.4 = f32[16,2,8192]{2,1,0:T(2,128)S(1)} dynamic-update-slice(f32[16,2,8192]{2,1,0:T(2,128)S(1)} %get-tuple-element.111, f32[16,2,128]{2,1,0:T(2,128)S(1)} %fusion.336, s32[]{:T(128)} %constant.113.clone.1..sunk, s32[]{:T(128)} %constant.113.clone.1..sunk, s32[]{:T(128)S(6)} %select_n.325) | dynamic-update-slice | bytes 32772 | tf_op jit(solution)/shard_map/while/body/eval_jaxpr/dynamic_update_slice | solution.py:159
  181.6 2.5 %dynamic_update_slice.4 = f32[16,2,8192]{2,1,0:T(2,128)S(1)} dynamic-update-slice(f32[16,2,8192]{2,1,0:T(2,128)S(1)} %get-tuple-element.111, f32[16,2,128]{2,1,0:T(2,128)S(1)} %fusion.336, s32[]{:T(128)} %constant.113.clone.1..sunk, s32[]{:T(128)} %constant.113.clone.1..sunk, s32[]{:T(128)S(6)} %select_n.325) | dynamic-update-slice | bytes 32772 | tf_op jit(solution)/shard_map/while/body/eval_jaxpr/dynamic_update_slice | solution.py:159
  186.8 2.5 %dynamic_update_slice.4 = f32[16,2,8192]{2,1,0:T(2,128)S(1)} dynamic-update-slice(f32[16,2,8192]{2,1,0:T(2,128)S(1)} %get-tuple-element.111, f32[16,2,128]{2,1,0:T(2,128)S(1)} %fusion.336, s32[]{:T(128)} %constant.113.clone.1..sunk, s32[]{:T(128)} %constant.113.clone.1..sunk, s32[]{:T(128)S(6)} %select_n.325) | dynamic-update-slice | bytes 32772 | tf_op jit(solution)/shard_map/while/body/eval_jaxpr/dynamic_update_slice | solution.py:159
  189.7 1.4 slice_reduce_fusion
  191.3 0.7 fusion.101
  192.0 0.7 fusion.90
  192.9 0.7 convolution_subtract_fusion.2
  193.6 0.7 convolution_add_fusion.2
  194.4 1.7 fusion.25
  196.1 1.7 fusion.23
  197.8 1.7 fusion.16
  199.9 1.7 fusion.14
  201.9 1.3 maximum_multiply_fusion
  (99 shorter events, 18.2 us)
Async XLA Ops:
  1.7 1.2 copy-start.4
  15.8 4.4 %copy-start.1 = (f32[64,64,64]{2,1,0:T(8,128)S(1)}, f32[64,64,64]{2,1,0:T(8,128)}, u32[]{:S(2)}) copy-start(f32[64,64,64]{2,1,0:T(8,128)} %reshape_squeeze.13) | copy-start | bytes 3145732
  15.8 4.4 %copy-start.2 = (f32[64,64,64]{2,0,1:T(8,128)S(1)}, f32[64,64,64]{2,0,1:T(8,128)}, u32[]{:S(2)}) copy-start(f32[64,64,64]{2,0,1:T(8,128)} %fusion.95) | copy-start | bytes 3145732
  23.9 9.5 %copy-start = (f32[64,64,64]{2,0,1:T(8,128)S(1)}, f32[64,64,64]{2,0,1:T(8,128)}, u32[]{:S(2)}) copy-start(f32[64,64,64]{2,0,1:T(8,128)} %convolution_add_fusion) | copy-start | bytes 3145732
  64.4 3.5 %copy-start.3 = (f32[64,64,64]{0,2,1:T(8,128)S(1)}, f32[64,64,64]{0,2,1:T(8,128)}, u32[]{:S(2)}) copy-start(f32[64,64,64]{0,2,1:T(8,128)} %copy.141) | copy-start | bytes 3145732
  67.9 30.4 %copy-start.8 = (s32[8]{0:T(128)S(1)}, s32[8]{0:T(128)}, u32[]{:S(2)}) copy-start(s32[8]{0:T(128)} %param.11) | copy-start | bytes 100
  67.9 35.2 %copy-start.7 = (f32[128]{0:T(128)S(1)}, f32[128]{0:T(128)}, u32[]{:S(2)}) copy-start(f32[128]{0:T(128)} %param.10) | copy-start | bytes 1540
  98.3 10.2 %copy-start.6 = (f32[2,512]{1,0:T(2,128)S(1)}, f32[2,512]{1,0:T(2,128)}, u32[]{:S(2)}) copy-start(f32[2,512]{1,0:T(2,128)} %param.12) | copy-start | bytes 12292
  98.3 14.7 %copy-start.5 = (s32[2,2,512]{2,1,0:T(2,128)S(1)}, s32[2,2,512]{2,1,0:T(2,128)}, u32[]{:S(2)}) copy-start(s32[2,2,512]{2,1,0:T(2,128)} %param.13) | copy-start | bytes 24580
  104.2 14.1 %all-to-all-start = ((f32[16,4,2,2,128]{4,0,2,3,1:T(8,128)}), f32[16,4,2,2,128]{4,0,2,3,1:T(8,128)S(1)}, u32[]{:S(2)}, u32[]{:S(2)}) async-start(f32[16,4,2,2,128]{4,0,2,3,1:T(8,128)} %pad_maximum_fusion), calls=%async_computation | async-start | bytes 262144 | tf_op jit(solution)/shard_map/all_to_all | solution.py:190
  137.5 11.5 %all-to-all-start.2 = ((f32[4,4,4,2,2,128]{5,1,3,2,4,0:T(4,128)}), f32[4,4,4,2,2,128]{5,1,3,2,4,0:T(4,128)S(1)}, u32[]{:S(2)}, u32[]{:S(2)}) async-start(f32[4,4,4,2,2,128]{5,1,3,2,4,0:T(4,128)} %copy.125), calls=%async_computation.2 | async-start | bytes 262144 | tf_op jit(solution)/shard_map/all_to_all | solution.py:196
where the time goes:
time: 207 us; the launch traced here: 203 us
  matrix products  72.1 us (35%)
  local copies, waits for them, and re-layouts  48 us (23%)
  other arithmetic  34.6 us (17%)
  blocking collectives  16.7 us (8%)
  loops' own time  15.9 us (8%)
  starting transfers between devices  9.78 us (5%)
  waiting for transfers between devices  5.68 us (3%)
    concatenate x1, other arithmetic, facet_blocks(): doubled = jnp.concatenate([spectrum, spectrum], axis=2)  30.4 us
    dynamic_update_slice x8, local copies, waits for them, and re-layouts, add_subgrid(): lax.dynamic_update_slice_in_dim(running, current + seg_rows, offset_one, 2)  18 us
    another operation x1, loops' own time, facet_image(): doubled, unused = lax.scan(add_subgrid, initial, (joined, offsets_here))  15.9 us
    dot_general x2, matrix products, factored_transform(): jnp.einsum('...kb,bm->...mk', real_t, sin_b, precision=exact_mode)  11.5 us
    dot_general x2, matrix products, factored_transform(): jnp.einsum('...kb,bm->...mk', real_t, cos_b, precision=exact_mode)  11.5 us
    dot_general x2, matrix products, factored_transform(): jnp.einsum('...kb,bm->...mk', imag_t, sin_b, precision=exact_mode)  11.2 us
    dot_general x2, matrix products, factored_transform(): jnp.einsum('...kb,bm->...mk', imag_t, cos_b, precision=exact_mode)  9.33 us
    all_to_all x1, blocking collectives, on_device(): lax.all_to_all(summed, 'facet', split_axis=2, concat_axis=2, tiled=True)  7.73 us
  transfers between devices with their start and end apart: 2, of which 1 were waited for; matrix products, arithmetic and copies ran while one was open for 1% of the time, Pallas kernels for 0%

commit v1 on v0

v1 whole, which is shorter than its diff:
```python
import functools
import math

import jax
import jax.numpy as jnp
import numpy as np
from jax import lax
from jax.experimental import pallas as pl
from jax.experimental.pallas import tpu as pltpu
from jax.sharding import PartitionSpec as P

MESH = pl.DeviceIdType.MESH
F32 = jnp.float32
BF16 = jnp.bfloat16


def complex_rows(matrix):
    return np.block([[matrix.real, matrix.imag], [-matrix.imag, matrix.real]])


def tables(length, width, facet_count):
    low = length // width
    quads = width // low
    a = np.arange(width)
    b = np.arange(low)
    dft = np.exp(-2j * np.pi * np.outer(a, a) / width)
    order = (a.reshape(width // quads, quads).T).reshape(-1)
    picked = dft[:, order]
    spread = np.zeros((2, width, width, 2))
    spread[0, :, :, 0] = picked.real
    spread[0, :, :, 1] = -picked.imag
    spread[1, :, :, 0] = picked.imag
    spread[1, :, :, 1] = picked.real
    outer = spread.reshape(2 * width, 2 * width)
    turn = np.tile(np.exp(-2j * np.pi * np.outer(a, b) / length), (1, quads))
    turn = np.stack([turn.real, turn.imag]).astype(np.float32)
    fine = np.exp(-2j * np.pi * np.outer(b, b) / low) * length**-0.5
    pick = np.zeros((low, 2, quads, 2, quads, low))
    for quad in range(quads):
        pick[:, 0, quad, 0, quad] = fine.real
        pick[:, 0, quad, 1, quad] = -fine.imag
        pick[:, 1, quad, 0, quad] = fine.imag
        pick[:, 1, quad, 1, quad] = fine.real
    pick = pick.reshape(low, 2 * quads, 2 * width).astype(np.float32)
    unit = complex_rows(np.conj(dft) * width**-0.5)
    twist = np.exp(-2j * np.pi * np.outer(np.arange(facet_count), a) / (facet_count * width))
    twist = np.stack([twist.real, twist.imag]).astype(np.float32)
    outer, unit = outer.astype(np.float32), unit.astype(np.float32)
    return outer, outer.T, turn, pick, unit, unit.T, twist


def split(value):
    high = value.astype(BF16)
    return high, (value - high.astype(F32)).astype(BF16)


def mm(left, right, transposed=False):
    dims = (((1,), (1 if transposed else 0,)), ((), ()))
    dot = functools.partial(lax.dot_general, dimension_numbers=dims, preferred_element_type=F32)
    return dot(left[0], right[0]) + (dot(left[0], right[1]) + dot(left[1], right[0]))


def radix(parts, sign):
    count = len(parts)
    if count == 1:
        return parts
    if count % 2:
        raise ValueError("odd length")
    even = radix(parts[0::2], sign)
    odd = radix(parts[1::2], sign)
    first, second = [], []
    for k in range(count // 2):
        real, imag = odd[k]
        if 4 * k == count:
            real, imag = (-imag, real) if sign > 0 else (imag, -real)
        elif k:
            c = math.cos(2 * math.pi * k / count)
            s = sign * math.sin(2 * math.pi * k / count)
            real, imag = real * c - imag * s, real * s + imag * c
        first.append((even[k][0] + real, even[k][1] + imag))
        second.append((even[k][0] - real, even[k][1] - imag))
    return first + second


def swap_blocks(blocks, low):
    quads = len(blocks)
    group = lax.broadcasted_iota(jnp.int32, blocks[0].shape, 1) // low
    width = quads * low
    out = []
    for i in range(quads):
        total = None
        for j in range(quads):
            shift = ((j - i) * low) % width
            moved = pltpu.roll(blocks[j], shift, 1) if shift else blocks[j]
            total = moved if total is None else jnp.where(group == j, moved, total)
        out.append(total)
    return out


def kernel(
    geometry,
    offsets_ref,
    facets_ref,
    correction_ref,
    window_ref,
    phases_ref,
    coverage_ref,
    outer_ref,
    outer_t_ref,
    turn_ref,
    pick_ref,
    unit_ref,
    unit_t_ref,
    twist_ref,
    out_ref,
    image,
    gain,
    cut,
    sent,
    arrived,
    back,
    returned,
    segments,
    counts,
    expanded,
    screens,
    load_sem,
    fwd_send,
    fwd_recv,
    bwd_send,
    bwd_recv,
    cov_send,
    cov_recv,
    ph_send,
    ph_recv,
):
    facet_count, sub_count, pair_count = geometry
    facet = lax.axis_index("facet")
    sub = lax.axis_index("sub")
    pair = lax.axis_index("wa")
    rows = image.shape[0]
    width = window_ref.shape[1]
    subs = offsets_ref.shape[0]
    low = pick_ref.shape[0]
    quads = width // low
    length = low * width
    span = subs * quads
    per_sub, per_wa = coverage_ref.shape[0], coverage_ref.shape[1]
    planes = per_wa * pair_count
    total = facet_count * width

    unit, unit_t = split(unit_ref[...]), split(unit_t_ref[...])

    facet_mates = [lax.rem(facet + d, facet_count) for d in range(1, facet_count)]
    hops = [(ds, dw) for ds in range(sub_count) for dw in range(pair_count) if ds or dw]
    barrier = pltpu.get_barrier_semaphore()
    for mate in facet_mates:
        pl.semaphore_signal(barrier, inc=1, device_id={"facet": mate}, device_id_type=MESH)
    grid_mates = [(lax.rem(sub + ds, sub_count), lax.rem(pair + dw, pair_count)) for ds, dw in hops]
    for mate_sub, mate_pair in grid_mates:
        pl.semaphore_signal(
            barrier, inc=1, device_id={"sub": mate_sub, "wa": mate_pair}, device_id_type=MESH
        )
    load = pltpu.make_async_copy(
        facets_ref.at[pl.ds((sub * pair_count + pair) * rows, rows)], image, load_sem
    )
    load.start()

    gain[pl.ds(0, low, stride=2), :] = correction_ref[...]
    gain[pl.ds(1, low, stride=2), :] = correction_ref[...]
    lane = lax.broadcasted_iota(jnp.int32, (1, width), 1)
    starts = [offsets_ref[s] for s in range(subs)]
    first_q = [start // width for start in starts]
    rests = [start - q * width for start, q in zip(starts, first_q)]
    rows_of = lax.broadcasted_iota(jnp.int32, (span, width), 0) // quads
    offset_rows = jnp.zeros((span, width), jnp.int32)
    for s in range(subs):
        offset_rows = jnp.where(rows_of == s, rests[s], offset_rows)
    span_lane = lax.broadcasted_iota(jnp.int32, (span, width), 1)
    angle = lax.rem(offset_rows * span_lane, width).astype(F32) * (2.0 * math.pi / width)
    turn_cos, turn_sin = jnp.cos(angle), jnp.sin(angle)
    is_first = span_lane >= offset_rows
    window_full = jnp.broadcast_to(window_ref[...], (8, width))
    window_rows = jnp.zeros((span, width), F32)
    for s in range(subs):
        moved = pltpu.roll(window_full, rests[s], 1)[0:1]
        window_rows = jnp.where(rows_of == s, moved, window_rows)
    picked = []
    for s in range(subs):
        picked.append(pick_ref[first_q[s]])
        picked.append(pick_ref[lax.rem(first_q[s] + 1, low)])
    picked = split(jnp.concatenate(picked, axis=0))

    load.wait()
    gains = gain[...]
    groups = []
    for g in range(facet_count):
        blocks = [image[g * quads + i] * gains for i in range(quads)]
        groups.append(jnp.concatenate(swap_blocks(blocks, low), axis=0))
    spread = jnp.concatenate(groups, axis=1)
    mixed = mm(split(outer_ref[...]), split(spread))
    table_cos, table_sin = turn_ref[0], turn_ref[1]
    turned = []
    for g in range(facet_count):
        real = mixed[:width, g * width : (g + 1) * width]
        imag = mixed[width:, g * width : (g + 1) * width]
        turned.append(
            jnp.concatenate(
                [real * table_cos - imag * table_sin, real * table_sin + imag * table_cos], axis=1
            )
        )
    turned = jnp.concatenate(turned, axis=0)
    spectrum = mm(picked, split(turned), transposed=True)

    pl.semaphore_wait(barrier, len(facet_mates) + len(hops))
    copies = []
    for i, (mate_sub, mate_pair) in enumerate(grid_mates):
        copy = pltpu.make_async_remote_copy(
            src_ref=coverage_ref,
            dst_ref=counts.at[sub, pair],
            send_sem=cov_send.at[i],
            recv_sem=cov_recv.at[i],
            device_id={"sub": mate_sub, "wa": mate_pair},
            device_id_type=MESH,
        )
        copy.start()
        copies.append(copy)
    counts[sub, pair] = coverage_ref[...]
    for d in range(1, pair_count):
        copy = pltpu.make_async_remote_copy(
            src_ref=phases_ref,
            dst_ref=screens.at[pair],
            send_sem=ph_send.at[d - 1],
            recv_sem=ph_recv.at[d - 1],
            device_id={"wa": lax.rem(pair + d, pair_count)},
            device_id_type=MESH,
        )
        copy.start()
        copies.append(copy)
    screens[pair] = phases_ref[...]

    for s in range(subs):
        here = slice(s * quads, (s + 1) * quads)
        base = s * 4 * quads
        keep = is_first[here]
        win = window_rows[here]
        for g in range(facet_count):
            cols = slice(g * width, (g + 1) * width)
            for c in range(2):
                one = spectrum[base + c * quads : base + (c + 1) * quads, cols]
                two = spectrum[base + (2 + c) * quads : base + (3 + c) * quads, cols]
                cut[g, here, c * width : (c + 1) * width] = jnp.where(keep, one, two) * win
    mixed = mm(split(cut[...].reshape(facet_count * span, 2 * width)), unit)
    for g in range(facet_count):
        real = mixed[g * span : (g + 1) * span, :width]
        imag = mixed[g * span : (g + 1) * span, width:]
        sent[g, :, :width] = real * turn_cos + imag * turn_sin
        sent[g, :, width:] = imag * turn_cos - real * turn_sin
    forward = []
    for i, mate in enumerate(facet_mates):
        copy = pltpu.make_async_remote_copy(
            src_ref=sent.at[mate],
            dst_ref=arrived.at[facet],
            send_sem=fwd_send.at[i],
            recv_sem=fwd_recv.at[i],
            device_id={"facet": mate},
            device_id_type=MESH,
        )
        copy.start()
        forward.append(copy)
    arrived[facet] = sent[facet]

    for copy in copies:
        copy.wait()
    for owner in range(sub_count):
        for p in range(pair_count):
            for i in range(per_sub):
                for j in range(per_wa):
                    at = (p * per_wa + j) * span + (owner * per_sub + i) * quads
                    row = counts[owner, p, i, j : j + 1].astype(F32)
                    expanded[at : at + quads, :] = jnp.broadcast_to(row, (quads, total))
    source = lax.broadcasted_iota(jnp.int32, (total, total), 0)
    target = lax.broadcasted_iota(jnp.int32, (total, total), 1)
    wanted = lax.rem(target, width) * facet_count + target // width
    chooser = jnp.where(source == wanted, 1.0, 0.0).astype(BF16)
    weights = jnp.dot(expanded[...].astype(BF16), chooser, preferred_element_type=F32)
    weights = weights * (1.0 / (facet_count * planes))
    kernels = []
    for p in range(pair_count):
        screen = screens[p]
        cos_all, sin_all = jnp.cos(screen), jnp.sin(screen)
        for j in range(per_wa):
            kernels.append((cos_all[j : j + 1], sin_all[j : j + 1]))
    twist = [(twist_ref[0, k : k + 1], twist_ref[1, k : k + 1]) for k in range(facet_count)]

    for copy in forward:
        copy.wait()
    pieces = [[] for _ in range(facet_count)]
    for w in range(planes):
        parts = []
        for f in range(facet_count):
            cols = slice(f * width, (f + 1) * width)
            kc, ks = kernels[w][0][:, cols], kernels[w][1][:, cols]
            real, imag = arrived[f, :, :width], arrived[f, :, width:]
            parts.append((real * kc - imag * ks, real * ks + imag * kc))
        for k, (real, imag) in enumerate(radix(parts, -1)):
            tc, ts = twist[k]
            pieces[k].append(
                jnp.concatenate([real * tc - imag * ts, real * ts + imag * tc], axis=1)
            )
    stacked = jnp.concatenate([piece for group in pieces for piece in group], axis=0)
    grid = mm(split(stacked), unit_t)
    scale = jnp.concatenate(
        [weights[:, k * width : (k + 1) * width] for k in range(facet_count)], axis=0
    )
    weighted = grid * jnp.concatenate([scale, scale], axis=1)
    image_side = mm(split(weighted), unit)
    sums = [None] * facet_count
    for w in range(planes):
        parts = []
        for k in range(facet_count):
            at = (k * planes + w) * span
            real = image_side[at : at + span, :width]
            imag = image_side[at : at + span, width:]
            tc, ts = twist[k]
            parts.append((real * tc + imag * ts, imag * tc - real * ts))
        for f, (real, imag) in enumerate(radix(parts, 1)):
            cols = slice(f * width, (f + 1) * width)
            kc, ks = kernels[w][0][:, cols], kernels[w][1][:, cols]
            term = (real * kc + imag * ks, imag * kc - real * ks)
            sums[f] = term if w == 0 else (sums[f][0] + term[0], sums[f][1] + term[1])
    for f in range(facet_count):
        back[f, :, :width] = sums[f][0]
        back[f, :, width:] = sums[f][1]
    backward = []
    for i, mate in enumerate(facet_mates):
        copy = pltpu.make_async_remote_copy(
            src_ref=back.at[mate],
            dst_ref=returned.at[facet],
            send_sem=bwd_send.at[i],
            recv_sem=bwd_recv.at[i],
            device_id={"facet": mate},
            device_id_type=MESH,
        )
        copy.start()
        backward.append(copy)
    returned[facet] = back[facet]
    for copy in backward:
        copy.wait()

    unturned = []
    for g in range(facet_count):
        real, imag = returned[g, :, :width], returned[g, :, width:]
        unturned.append(
            jnp.concatenate(
                [real * turn_cos - imag * turn_sin, real * turn_sin + imag * turn_cos], axis=1
            )
        )
    unturned = jnp.concatenate(unturned, axis=0)
    mixed = mm(split(unturned), unit_t)
    win_first = jnp.where(is_first, window_rows, 0.0)
    win_second = jnp.where(is_first, 0.0, window_rows)
    for g in range(facet_count):
        cols = slice(g * width, (g + 1) * width)
        for c in range(2):
            part = mixed[g * span : (g + 1) * span, c * width : (c + 1) * width]
            for h, win in enumerate((win_first, win_second)):
                masked = part * win
                for s in range(subs):
                    at = (4 * s + 2 * h + c) * quads
                    segments[at : at + quads, cols] = masked[s * quads : (s + 1) * quads]
    columns = jnp.concatenate(
        [segments[:, g * width : (g + 1) * width].T for g in range(facet_count)], axis=0
    )
    fine = mm(split(columns), picked)
    reals, imags = [], []
    for g in range(facet_count):
        real = fine[g * width : (g + 1) * width, :width]
        imag = fine[g * width : (g + 1) * width, width:]
        reals.append(real * table_cos + imag * table_sin)
        imags.append(imag * table_cos - real * table_sin)
    joined = jnp.concatenate(
        [jnp.concatenate(reals, axis=1), jnp.concatenate(imags, axis=1)], axis=0
    )
    spread = mm(split(outer_t_ref[...]), split(joined))
    part = 2 * width // quads
    for g in range(facet_count):
        cols = slice(g * width, (g + 1) * width)
        blocks = [spread[i * part : (i + 1) * part, cols] for i in range(quads)]
        for i, block in enumerate(swap_blocks(blocks, low)):
            out_ref[g * quads + i] = block * gains


def on_device(facets, correction, window, offsets, phases, coverage):
    facet_count = lax.axis_size("facet")
    sub_count = lax.axis_size("sub")
    pair_count = lax.axis_size("wa")
    row_count, length = facets.shape[1], facets.shape[3]
    width = window.shape[0]
    subs = offsets.shape[0]
    rows = row_count // (sub_count * pair_count)
    low = length // width
    quads = width // low
    if rows != facet_count * quads or low * quads != width:
        raise ValueError("unsupported sizes")
    span = subs * quads
    total = facet_count * width
    lines = length // width
    image = facets.reshape(row_count, 2, lines, width)
    image = jnp.transpose(image, (0, 2, 1, 3)).reshape(row_count, 2 * lines, width)
    constants = tables(length, width, facet_count)
    vmem = pl.BlockSpec(memory_space=pltpu.VMEM)
    others = sub_count * pair_count - 1
    dma = pltpu.SemaphoreType.DMA
    block = (facet_count, span, 2 * width)
    result = pl.pallas_call(
        functools.partial(kernel, (facet_count, sub_count, pair_count)),
        out_shape=jax.ShapeDtypeStruct((rows, 2 * lines, width), F32),
        in_specs=[
            pl.BlockSpec(memory_space=pltpu.SMEM),
            pl.BlockSpec(memory_space=pl.ANY),
        ]
        + [vmem] * (4 + len(constants)),
        out_specs=vmem,
        scratch_shapes=[
            pltpu.VMEM((rows, 2 * lines, width), F32),
            pltpu.VMEM((2 * lines, width), F32),
            pltpu.VMEM(block, F32),
            pltpu.VMEM(block, F32),
            pltpu.VMEM(block, F32),
            pltpu.VMEM(block, F32),
            pltpu.VMEM(block, F32),
            pltpu.VMEM((4 * span, total), F32),
            pltpu.VMEM((sub_count, pair_count) + coverage.shape, jnp.int32),
            pltpu.VMEM((coverage.shape[1] * pair_count * span, total), F32),
            pltpu.VMEM((pair_count,) + phases.shape, F32),
            dma,
            dma((facet_count - 1,)),
            dma((facet_count - 1,)),
            dma((facet_count - 1,)),
            dma((facet_count - 1,)),
            dma((others,)),
            dma((others,)),
            dma((max(pair_count - 1, 1),)),
            dma((max(pair_count - 1, 1),)),
        ],
        compiler_params=pltpu.CompilerParams(
            collective_id=0, has_side_effects=True, vmem_limit_bytes=56 * 1024 * 1024
        ),
    )(
        offsets,
        image,
        correction.reshape(lines, width),
        window.reshape(1, width),
        phases,
        coverage,
        *[jnp.asarray(table) for table in constants],
    )
    result = jnp.transpose(result.reshape(rows, lines, 2, width), (0, 2, 1, 3))
    return result.reshape(1, rows, 2, length)


def solution(mesh):
    return jax.shard_map(
        on_device,
        mesh=mesh,
        in_specs=(
            P("facet", None, None, None),
            P("facet", None),
            P(),
            P(),
            P("wa", None),
            P("sub", "wa", None),
        ),
        out_specs=P("facet", ("sub", "wa"), None, None),
        check_vma=False,
    )
```

time: 207 us -> 21.2 us (0.10); the launches traced: 203 us -> 21 us
  matrix products: 72.1 us -> 0 us
  local copies, waits for them, and re-layouts: 48 us -> 1.89 us
  other arithmetic: 34.6 us -> 0 us
  Pallas kernels: 0 us -> 19.1 us
  blocking collectives: 16.7 us -> 0 us
  loops' own time: 15.9 us -> 0 us
  starting transfers between devices: 9.78 us -> 0 us
  waiting for transfers between devices: 5.68 us -> 0 us
    dot_general x34 -> x0, matrix products: 72.1 us -> none  [the longest x2 11.5 us: factored_transform(): jnp.einsum('...kb,bm->...mk', real_t, sin_b, precision=exact_mode)]
    concatenate x2 -> x0, other arithmetic: 30.5 us -> none  [the longest x1 30.4 us: facet_blocks(): doubled = jnp.concatenate([spectrum, spectrum], axis=2)]
    pallas_call x0 -> x1, Pallas kernels: none -> 19.1 us  [on_device(): pl.pallas_call(functools.partial(kernel, (facet_count, sub_count, pair_co...]
    dynamic_update_slice x8 -> x0, local copies, waits for them, and re-layouts: 18 us -> none  [add_subgrid(): lax.dynamic_update_slice_in_dim(running, current + seg_rows, offset_one, 2)]
    another operation x1 -> x0, loops' own time: 15.9 us -> none  [facet_image(): doubled, unused = lax.scan(add_subgrid, initial, (joined, offsets_here))]
    all_to_all x2 -> x0, starting transfers between devices: 9.78 us -> none  [the longest x1 5.57 us: on_device(): lax.all_to_all(returned, 'sub', split_axis=0, concat_axis=3, tiled=True)]
    all_gather x2 -> x0, blocking collectives: 8.93 us -> none  [the longest x1 4.54 us: on_device(): lax.all_gather(coverage.astype(jnp.float32), 'wa', axis=1, tiled=True)]
    dynamic_slice x18 -> x0, local copies, waits for them, and re-layouts: 7.78 us -> none  [the longest x16 4.84 us: facet_image(): doubled, unused = lax.scan(add_subgrid, initial, (joined, offsets_here))]
  transfers between devices with their start and end apart: 2 -> 0, of which waited for: 1 -> 0; matrix products, arithmetic and copies ran while one was open for 1% -> 0% of each run, Pallas kernels for 0% -> 0%
where the time goes in v1:
time: 21.2 us; the launch traced here: 21 us
  Pallas kernels  19.1 us (90%)
  local copies, waits for them, and re-layouts  1.89 us (9%)
    pallas_call x1, Pallas kernels, on_device(): pl.pallas_call(functools.partial(kernel, (facet_count, sub_count, pair_co...  19.1 us
    unnamed x1, local copies, waits for them, and re-layouts  1.89 us

profile of v1, /device:TPU:0, one launch (start us, length us, event | category | flops | bytes accessed | tf_op | source)
XLA Modules:
  0.0 21.0 jit_solution(5065005218092593217)
XLA Ops:
  0.0 19.1 %shard_map.127 = f32[16,64,128]{2,1,0:T(8,128)} custom-call(s32[8]{0:T(128)} %offsets_ref.1, f32[128,64,128]{2,1,0:T(8,128)} %bitcast.12, f32[32,128]{1,0:T(8,128)} %bitcast.14, f32[1,128]{1,0:T(1,128)} %bitcast.15, f32[2,512]{1,0:T(2,128)} %phases_ref.1, s32[2,2,512]{2,1,0:T(2,128)} %coverage_ref.1, f32[256,256]{1,0:T(8,128)} %constant.14.clone.outer_ref, ...), custom_call_target="tpu_custom_call" | custom-call | tf_op jit(solution)/shard_map/pallas_call | solution.py:416
  19.1 1.9 %copy.17 = f32[1,16,2,4096]{3,2,1,0:T(2,128)} copy(f32[1,16,2,4096]{3,2,1,0:T(2,128)} %bitcast.13) | data formatting | bytes 1048576

commit v2 on v1

--- a/solution.py
+++ b/solution.py
@@ -46,7 +46,7 @@
     twist = np.exp(-2j * np.pi * np.outer(np.arange(facet_count), a) / (facet_count * width))
     twist = np.stack([twist.real, twist.imag]).astype(np.float32)
     outer, unit = outer.astype(np.float32), unit.astype(np.float32)
-    return outer, outer.T, turn, pick, unit, unit.T, twist
+    return twist, outer, turn, pick, unit, unit.T, outer.T
 
 
 def split(value):
@@ -58,6 +58,22 @@
     dims = (((1,), (1 if transposed else 0,)), ((), ()))
     dot = functools.partial(lax.dot_general, dimension_numbers=dims, preferred_element_type=F32)
     return dot(left[0], right[0]) + (dot(left[0], right[1]) + dot(left[1], right[0]))
+
+
+def cos_sin(value):
+    turns = jnp.floor(value * (2.0 / math.pi) + 0.5)
+    rest = (value - turns * 1.5703125) - turns * (math.pi / 2 - 1.5703125)
+    square = rest * rest
+    sine = rest + rest * square * (
+        -1.0 / 6 + square * (1.0 / 120 + square * (-1.0 / 5040 + square * (1.0 / 362880)))
+    )
+    cosine = 1.0 + square * (
+        -0.5 + square * (1.0 / 24 + square * (-1.0 / 720 + square * (1.0 / 40320)))
+    )
+    odd = jnp.abs(turns) == 1.0
+    sign_cos = jnp.where(turns == 1.0, -1.0, jnp.where(jnp.abs(turns) == 2.0, -1.0, 1.0))
+    sign_sin = jnp.where(turns == -1.0, -1.0, jnp.where(jnp.abs(turns) == 2.0, -1.0, 1.0))
+    return jnp.where(odd, sine, cosine) * sign_cos, jnp.where(odd, cosine, sine) * sign_sin
 
 
 def radix(parts, sign):
@@ -83,18 +99,22 @@
 
 
 def swap_blocks(blocks, low):
-    quads = len(blocks)
-    group = lax.broadcasted_iota(jnp.int32, blocks[0].shape, 1) // low
-    width = quads * low
-    out = []
-    for i in range(quads):
-        total = None
-        for j in range(quads):
-            shift = ((j - i) * low) % width
-            moved = pltpu.roll(blocks[j], shift, 1) if shift else blocks[j]
-            total = moved if total is None else jnp.where(group == j, moved, total)
-        out.append(total)
-    return out
+    blocks = list(blocks)
+    count = len(blocks)
+    width = count * low
+    lane = lax.broadcasted_iota(jnp.int32, blocks[0].shape, 1)
+    step = count // 2
+    while step:
+        shift = step * low
+        upper = (lane & shift) != 0
+        for i in range(count):
+            if i & step:
+                continue
+            one, two = blocks[i], blocks[i + step]
+            blocks[i] = jnp.where(upper, pltpu.roll(two, shift, 1), one)
+            blocks[i + step] = jnp.where(upper, two, pltpu.roll(one, width - shift, 1))
+        step //= 2
+    return blocks
 
 
 def kernel(
@@ -105,13 +125,13 @@
     window_ref,
     phases_ref,
     coverage_ref,
-    outer_ref,
-    outer_t_ref,
-    turn_ref,
-    pick_ref,
-    unit_ref,
-    unit_t_ref,
     twist_ref,
+    outer_far,
+    turn_far,
+    pick_far,
+    unit_far,
+    unit_t_far,
+    outer_t_far,
     out_ref,
     image,
     gain,
@@ -133,6 +153,13 @@
     cov_recv,
     ph_send,
     ph_recv,
+    outer_ref,
+    turn_ref,
+    pick_ref,
+    unit_ref,
+    unit_t_ref,
+    outer_t_ref,
+    table_sem,
 ):
     facet_count, sub_count, pair_count = geometry
     facet = lax.axis_index("facet")
@@ -149,8 +176,6 @@
     planes = per_wa * pair_count
     total = facet_count * width
 
-    unit, unit_t = split(unit_ref[...]), split(unit_t_ref[...])
-
     facet_mates = [lax.rem(facet + d, facet_count) for d in range(1, facet_count)]
     hops = [(ds, dw) for ds in range(sub_count) for dw in range(pair_count) if ds or dw]
     barrier = pltpu.get_barrier_semaphore()
@@ -165,26 +190,39 @@
         facets_ref.at[pl.ds((sub * pair_count + pair) * rows, rows)], image, load_sem
     )
     load.start()
+    fetches = {}
+    for i, (name, far, near) in enumerate(
+        (
+            ("outer", outer_far, outer_ref),
+            ("turn", turn_far, turn_ref),
+            ("pick", pick_far, pick_ref),
+            ("unit", unit_far, unit_ref),
+            ("unit_t", unit_t_far, unit_t_ref),
+            ("outer_t", outer_t_far, outer_t_ref),
+        )
+    ):
+        fetches[name] = pltpu.make_async_copy(far, near, table_sem.at[i])
+        fetches[name].start()
 
     gain[pl.ds(0, low, stride=2), :] = correction_ref[...]
     gain[pl.ds(1, low, stride=2), :] = correction_ref[...]
-    lane = lax.broadcasted_iota(jnp.int32, (1, width), 1)
     starts = [offsets_ref[s] for s in range(subs)]
     first_q = [start // width for start in starts]
-    rests = [start - q * width for start, q in zip(starts, first_q)]
-    rows_of = lax.broadcasted_iota(jnp.int32, (span, width), 0) // quads
+    rests = [start & (width - 1) for start in starts]
+    row = lax.broadcasted_iota(jnp.int32, (span, width), 0)
     offset_rows = jnp.zeros((span, width), jnp.int32)
     for s in range(subs):
-        offset_rows = jnp.where(rows_of == s, rests[s], offset_rows)
+        offset_rows = jnp.where(row >= s * quads, rests[s], offset_rows)
     span_lane = lax.broadcasted_iota(jnp.int32, (span, width), 1)
-    angle = lax.rem(offset_rows * span_lane, width).astype(F32) * (2.0 * math.pi / width)
-    turn_cos, turn_sin = jnp.cos(angle), jnp.sin(angle)
+    steps = ((offset_rows * span_lane + width // 2) & (width - 1)) - width // 2
+    turn_cos, turn_sin = cos_sin(steps.astype(F32) * (2.0 * math.pi / width))
     is_first = span_lane >= offset_rows
     window_full = jnp.broadcast_to(window_ref[...], (8, width))
     window_rows = jnp.zeros((span, width), F32)
     for s in range(subs):
         moved = pltpu.roll(window_full, rests[s], 1)[0:1]
-        window_rows = jnp.where(rows_of == s, moved, window_rows)
+        window_rows = jnp.where(row >= s * quads, moved, window_rows)
+    fetches["pick"].wait()
     picked = []
     for s in range(subs):
         picked.append(pick_ref[first_q[s]])
@@ -198,7 +236,9 @@
         blocks = [image[g * quads + i] * gains for i in range(quads)]
         groups.append(jnp.concatenate(swap_blocks(blocks, low), axis=0))
     spread = jnp.concatenate(groups, axis=1)
+    fetches["outer"].wait()
     mixed = mm(split(outer_ref[...]), split(spread))
+    fetches["turn"].wait()
     table_cos, table_sin = turn_ref[0], turn_ref[1]
     turned = []
     for g in range(facet_count):
@@ -250,6 +290,8 @@
                 one = spectrum[base + c * quads : base + (c + 1) * quads, cols]
                 two = spectrum[base + (2 + c) * quads : base + (3 + c) * quads, cols]
                 cut[g, here, c * width : (c + 1) * width] = jnp.where(keep, one, two) * win
+    fetches["unit"].wait()
+    unit = split(unit_ref[...])
     mixed = mm(split(cut[...].reshape(facet_count * span, 2 * width)), unit)
     for g in range(facet_count):
         real = mixed[g * span : (g + 1) * span, :width]
@@ -270,6 +312,10 @@
         forward.append(copy)
     arrived[facet] = sent[facet]
 
+    fetches["unit_t"].wait()
+    unit_t = split(unit_t_ref[...])
+    fetches["outer_t"].wait()
+
     for copy in copies:
         copy.wait()
     for owner in range(sub_count):
@@ -280,15 +326,15 @@
                     row = counts[owner, p, i, j : j + 1].astype(F32)
                     expanded[at : at + quads, :] = jnp.broadcast_to(row, (quads, total))
     source = lax.broadcasted_iota(jnp.int32, (total, total), 0)
-    target = lax.broadcasted_iota(jnp.int32, (total, total), 1)
-    wanted = lax.rem(target, width) * facet_count + target // width
+    inner = lax.broadcasted_iota(jnp.int32, (1, width), 1) * facet_count
+    wanted = jnp.concatenate([inner + k for k in range(facet_count)], axis=1)
     chooser = jnp.where(source == wanted, 1.0, 0.0).astype(BF16)
     weights = jnp.dot(expanded[...].astype(BF16), chooser, preferred_element_type=F32)
     weights = weights * (1.0 / (facet_count * planes))
     kernels = []
     for p in range(pair_count):
         screen = screens[p]
-        cos_all, sin_all = jnp.cos(screen), jnp.sin(screen)
+        cos_all, sin_all = cos_sin(screen)
         for j in range(per_wa):
             kernels.append((cos_all[j : j + 1], sin_all[j : j + 1]))
     twist = [(twist_ref[0, k : k + 1], twist_ref[1, k : k + 1]) for k in range(facet_count)]
@@ -420,7 +466,8 @@
             pl.BlockSpec(memory_space=pltpu.SMEM),
             pl.BlockSpec(memory_space=pl.ANY),
         ]
-        + [vmem] * (4 + len(constants)),
+        + [vmem] * 5
+        + [pl.BlockSpec(memory_space=pl.ANY)] * (len(constants) - 1),
         out_specs=vmem,
         scratch_shapes=[
             pltpu.VMEM((rows, 2 * lines, width), F32),
@@ -443,7 +490,9 @@
             dma((others,)),
             dma((max(pair_count - 1, 1),)),
             dma((max(pair_count - 1, 1),)),
-        ],
+        ]
+        + [pltpu.VMEM(table.shape, F32) for table in constants[1:]]
+        + [dma((len(constants) - 1,))],
         compiler_params=pltpu.CompilerParams(
             collective_id=0, has_side_effects=True, vmem_limit_bytes=56 * 1024 * 1024
         ),

time: 21.2 us -> 20.9 us (0.986)
  Pallas kernels: 19.1 us -> 18.8 us
    pallas_call x1, Pallas kernels: 19.1 us -> 18.8 us  [on_device(): pl.pallas_call(functools.partial(kernel, (facet_count, sub_count, pair_co...]
where the time goes in v2:
time: 20.9 us; the launch traced here: 20.7 us
  Pallas kernels  18.8 us (90%)
  local copies, waits for them, and re-layouts  1.89 us (9%)
    pallas_call x1, Pallas kernels, on_device(): pl.pallas_call(functools.partial(kernel, (facet_count, sub_count, pair_co...  18.8 us
    unnamed x1, local copies, waits for them, and re-layouts  1.89 us

profile of v2, /device:TPU:0, one launch (start us, length us, event | category | flops | bytes accessed | tf_op | source)
XLA Modules:
  0.0 20.7 jit_solution(11113948642082109281)
XLA Ops:
  0.0 18.8 %shard_map.127 = f32[16,64,128]{2,1,0:T(8,128)} custom-call(s32[8]{0:T(128)} %offsets_ref.1, f32[128,64,128]{2,1,0:T(8,128)} %bitcast.12, f32[32,128]{1,0:T(8,128)} %bitcast.14, f32[1,128]{1,0:T(1,128)} %bitcast.15, f32[2,512]{1,0:T(2,128)} %phases_ref.1, s32[2,2,512]{2,1,0:T(2,128)} %coverage_ref.1, f32[2,4,128]{2,1,0:T(4,128)} %constant.14.clone.twist_ref, ...), custom_call_target="tpu_custom_call" | custom-call | tf_op jit(solution)/shard_map/pallas_call | solution.py:462
  18.8 1.9 %copy.17 = f32[1,16,2,4096]{3,2,1,0:T(2,128)} copy(f32[1,16,2,4096]{3,2,1,0:T(2,128)} %bitcast.13) | data formatting | bytes 1048576

commit v3 on v2

--- a/solution.py
+++ b/solution.py
@@ -117,6 +117,36 @@
     return blocks
 
 
+def offset_tables(offsets_ref, window_ref, quads):
+    width = window_ref.shape[1]
+    subs = offsets_ref.shape[0]
+    span = subs * quads
+    starts = [offsets_ref[s] for s in range(subs)]
+    first_q = [start // width for start in starts]
+    rests = [start & (width - 1) for start in starts]
+    row = lax.broadcasted_iota(jnp.int32, (span, width), 0)
+    offset_rows = jnp.zeros((span, width), jnp.int32)
+    window_full = jnp.broadcast_to(window_ref[...], (8, width))
+    window_rows = jnp.zeros((span, width), F32)
+    for s in range(subs):
+        offset_rows = jnp.where(row >= s * quads, rests[s], offset_rows)
+        moved = pltpu.roll(window_full, rests[s], 1)[0:1]
+        window_rows = jnp.where(row >= s * quads, moved, window_rows)
+    span_lane = lax.broadcasted_iota(jnp.int32, (span, width), 1)
+    steps = ((offset_rows * span_lane + width // 2) & (width - 1)) - width // 2
+    turn_cos, turn_sin = cos_sin(steps.astype(F32) * (2.0 * math.pi / width))
+    return first_q, turn_cos, turn_sin, span_lane >= offset_rows, window_rows
+
+
+def gather_pick(first_q, pick_ref):
+    low = pick_ref.shape[0]
+    picked = []
+    for q in first_q:
+        picked.append(pick_ref[q])
+        picked.append(pick_ref[lax.rem(q + 1, low)])
+    return split(jnp.concatenate(picked, axis=0))
+
+
 def kernel(
     geometry,
     offsets_ref,
@@ -131,16 +161,13 @@
     pick_far,
     unit_far,
     unit_t_far,
-    outer_t_far,
-    out_ref,
+    returned,
     image,
     gain,
     cut,
     sent,
     arrived,
     back,
-    returned,
-    segments,
     counts,
     expanded,
     screens,
@@ -158,7 +185,6 @@
     pick_ref,
     unit_ref,
     unit_t_ref,
-    outer_t_ref,
     table_sem,
 ):
     facet_count, sub_count, pair_count = geometry
@@ -198,7 +224,6 @@
             ("pick", pick_far, pick_ref),
             ("unit", unit_far, unit_ref),
             ("unit_t", unit_t_far, unit_t_ref),
-            ("outer_t", outer_t_far, outer_t_ref),
         )
     ):
         fetches[name] = pltpu.make_async_copy(far, near, table_sem.at[i])
@@ -206,28 +231,11 @@
 
     gain[pl.ds(0, low, stride=2), :] = correction_ref[...]
     gain[pl.ds(1, low, stride=2), :] = correction_ref[...]
-    starts = [offsets_ref[s] for s in range(subs)]
-    first_q = [start // width for start in starts]
-    rests = [start & (width - 1) for start in starts]
-    row = lax.broadcasted_iota(jnp.int32, (span, width), 0)
-    offset_rows = jnp.zeros((span, width), jnp.int32)
-    for s in range(subs):
-        offset_rows = jnp.where(row >= s * quads, rests[s], offset_rows)
-    span_lane = lax.broadcasted_iota(jnp.int32, (span, width), 1)
-    steps = ((offset_rows * span_lane + width // 2) & (width - 1)) - width // 2
-    turn_cos, turn_sin = cos_sin(steps.astype(F32) * (2.0 * math.pi / width))
-    is_first = span_lane >= offset_rows
-    window_full = jnp.broadcast_to(window_ref[...], (8, width))
-    window_rows = jnp.zeros((span, width), F32)
-    for s in range(subs):
-        moved = pltpu.roll(window_full, rests[s], 1)[0:1]
-        window_rows = jnp.where(row >= s * quads, moved, window_rows)
+    first_q, turn_cos, turn_sin, is_first, window_rows = offset_tables(
+        offsets_ref, window_ref, quads
+    )
     fetches["pick"].wait()
-    picked = []
-    for s in range(subs):
-        picked.append(pick_ref[first_q[s]])
-        picked.append(pick_ref[lax.rem(first_q[s] + 1, low)])
-    picked = split(jnp.concatenate(picked, axis=0))
+    picked = gather_pick(first_q, pick_ref)
 
     load.wait()
     gains = gain[...]
@@ -314,7 +322,6 @@
 
     fetches["unit_t"].wait()
     unit_t = split(unit_t_ref[...])
-    fetches["outer_t"].wait()
 
     for copy in copies:
         copy.wait()
@@ -394,6 +401,49 @@
     for copy in backward:
         copy.wait()
 
+
+def inverse_kernel(
+    offsets_ref,
+    returned,
+    correction_ref,
+    window_ref,
+    unit_t_far,
+    pick_far,
+    turn_far,
+    outer_t_far,
+    out_ref,
+    gain,
+    segments,
+    image,
+    unit_t_ref,
+    pick_ref,
+    turn_ref,
+    outer_t_ref,
+    table_sem,
+    out_sem,
+):
+    facet_count, span, double = returned.shape
+    width = double // 2
+    subs = offsets_ref.shape[0]
+    low = pick_ref.shape[0]
+    quads = width // low
+    fetches = {}
+    for i, (name, far, near) in enumerate(
+        (
+            ("unit_t", unit_t_far, unit_t_ref),
+            ("pick", pick_far, pick_ref),
+            ("turn", turn_far, turn_ref),
+            ("outer_t", outer_t_far, outer_t_ref),
+        )
+    ):
+        fetches[name] = pltpu.make_async_copy(far, near, table_sem.at[i])
+        fetches[name].start()
+    gain[pl.ds(0, low, stride=2), :] = correction_ref[...]
+    gain[pl.ds(1, low, stride=2), :] = correction_ref[...]
+    gains = gain[...]
+    first_q, turn_cos, turn_sin, is_first, window_rows = offset_tables(
+        offsets_ref, window_ref, quads
+    )
     unturned = []
     for g in range(facet_count):
         real, imag = returned[g, :, :width], returned[g, :, width:]
@@ -403,7 +453,8 @@
             )
         )
     unturned = jnp.concatenate(unturned, axis=0)
-    mixed = mm(split(unturned), unit_t)
+    fetches["unit_t"].wait()
+    mixed = mm(split(unturned), split(unit_t_ref[...]))
     win_first = jnp.where(is_first, window_rows, 0.0)
     win_second = jnp.where(is_first, 0.0, window_rows)
     for g in range(facet_count):
@@ -418,7 +469,10 @@
     columns = jnp.concatenate(
         [segments[:, g * width : (g + 1) * width].T for g in range(facet_count)], axis=0
     )
-    fine = mm(split(columns), picked)
+    fetches["pick"].wait()
+    fine = mm(split(columns), gather_pick(first_q, pick_ref))
+    fetches["turn"].wait()
+    table_cos, table_sin = turn_ref[0], turn_ref[1]
     reals, imags = [], []
     for g in range(facet_count):
         real = fine[g * width : (g + 1) * width, :width]
@@ -428,13 +482,22 @@
     joined = jnp.concatenate(
         [jnp.concatenate(reals, axis=1), jnp.concatenate(imags, axis=1)], axis=0
     )
+    fetches["outer_t"].wait()
     spread = mm(split(outer_t_ref[...]), split(joined))
     part = 2 * width // quads
+    stores = []
     for g in range(facet_count):
         cols = slice(g * width, (g + 1) * width)
         blocks = [spread[i * part : (i + 1) * part, cols] for i in range(quads)]
         for i, block in enumerate(swap_blocks(blocks, low)):
-            out_ref[g * quads + i] = block * gains
+            image[g * quads + i] = block * gains
+        store = pltpu.make_async_copy(
+            image.at[pl.ds(g * quads, quads)], out_ref.at[pl.ds(g * quads, quads)], out_sem.at[g]
+        )
+        store.start()
+        stores.append(store)
+    for store in stores:
+        store.wait()
 
 
 def on_device(facets, correction, window, offsets, phases, coverage):
@@ -454,20 +517,20 @@
     lines = length // width
     image = facets.reshape(row_count, 2, lines, width)
     image = jnp.transpose(image, (0, 2, 1, 3)).reshape(row_count, 2 * lines, width)
-    constants = tables(length, width, facet_count)
+    twist, outer, turn, pick, unit, unit_t, outer_t = tables(length, width, facet_count)
     vmem = pl.BlockSpec(memory_space=pltpu.VMEM)
+    smem = pl.BlockSpec(memory_space=pltpu.SMEM)
+    far = pl.BlockSpec(memory_space=pltpu.HBM)
     others = sub_count * pair_count - 1
     dma = pltpu.SemaphoreType.DMA
     block = (facet_count, span, 2 * width)
-    result = pl.pallas_call(
+    gains = correction.reshape(lines, width)
+    window = window.reshape(1, width)
+    first_tables = [outer, turn, pick, unit, unit_t]
+    returned = pl.pallas_call(
         functools.partial(kernel, (facet_count, sub_count, pair_count)),
-        out_shape=jax.ShapeDtypeStruct((rows, 2 * lines, width), F32),
-        in_specs=[
-            pl.BlockSpec(memory_space=pltpu.SMEM),
-            pl.BlockSpec(memory_space=pl.ANY),
-        ]
-        + [vmem] * 5
-        + [pl.BlockSpec(memory_space=pl.ANY)] * (len(constants) - 1),
+        out_shape=pltpu.VMEM(block, F32),
+        in_specs=[smem, far] + [vmem] * 5 + [far] * len(first_tables),
         out_specs=vmem,
         scratch_shapes=[
             pltpu.VMEM((rows, 2 * lines, width), F32),
@@ -476,8 +539,6 @@
             pltpu.VMEM(block, F32),
             pltpu.VMEM(block, F32),
             pltpu.VMEM(block, F32),
-            pltpu.VMEM(block, F32),
-            pltpu.VMEM((4 * span, total), F32),
             pltpu.VMEM((sub_count, pair_count) + coverage.shape, jnp.int32),
             pltpu.VMEM((coverage.shape[1] * pair_count * span, total), F32),
             pltpu.VMEM((pair_count,) + phases.shape, F32),
@@ -491,20 +552,27 @@
             dma((max(pair_count - 1, 1),)),
             dma((max(pair_count - 1, 1),)),
         ]
-        + [pltpu.VMEM(table.shape, F32) for table in constants[1:]]
-        + [dma((len(constants) - 1,))],
+        + [pltpu.VMEM(table.shape, F32) for table in first_tables]
+        + [dma((len(first_tables),))],
         compiler_params=pltpu.CompilerParams(
-            collective_id=0, has_side_effects=True, vmem_limit_bytes=56 * 1024 * 1024
+            collective_id=0, has_side_effects=True, vmem_limit_bytes=55 * 1024 * 1024
         ),
-    )(
-        offsets,
-        image,
-        correction.reshape(lines, width),
-        window.reshape(1, width),
-        phases,
-        coverage,
-        *[jnp.asarray(table) for table in constants],
-    )
+    )(offsets, image, gains, window, phases, coverage, jnp.asarray(twist), *map(jnp.asarray, first_tables))
+    second_tables = [unit_t, pick, turn, outer_t]
+    result = pl.pallas_call(
+        inverse_kernel,
+        out_shape=jax.ShapeDtypeStruct((rows, 2 * lines, width), F32),
+        in_specs=[smem] + [vmem] * 3 + [pl.BlockSpec(memory_space=pl.ANY)] * len(second_tables),
+        out_specs=far,
+        scratch_shapes=[
+            pltpu.VMEM((2 * lines, width), F32),
+            pltpu.VMEM((4 * span, total), F32),
+            pltpu.VMEM((rows, 2 * lines, width), F32),
+        ]
+        + [pltpu.VMEM(table.shape, F32) for table in second_tables]
+        + [dma((len(second_tables),)), dma((facet_count,))],
+        compiler_params=pltpu.CompilerParams(vmem_limit_bytes=48 * 1024 * 1024),
+    )(offsets, returned, gains, window, *map(jnp.asarray, second_tables))
     result = jnp.transpose(result.reshape(rows, lines, 2, width), (0, 2, 1, 3))
     return result.reshape(1, rows, 2, length)
 

time: 20.9 us -> 20.3 us (0.971)
  local copies, waits for them, and re-layouts: 1.89 us -> 0.03 us
  Pallas kernels: 18.8 us -> 20 us
    pallas_call x0 -> x1, Pallas kernels: none -> 3.44 us  [on_device(): pl.pallas_call(inverse_kernel, out_shape=jax.ShapeDtypeStruct((rows, 2 *...]
    pallas_call x1, Pallas kernels: 18.8 us -> 16.5 us  [on_device(): pl.pallas_call(functools.partial(kernel, (facet_count, sub_count, pair_co...]
    unnamed x1 -> x14, local copies, waits for them, and re-layouts: 1.89 us -> 0.03 us
where the time goes in v3:
time: 20.3 us; the launch traced here: 20.1 us
  Pallas kernels  20 us (99%)
    pallas_call x1, Pallas kernels, on_device(): pl.pallas_call(functools.partial(kernel, (facet_count, sub_count, pair_co...  16.5 us
    pallas_call x1, Pallas kernels, on_device(): pl.pallas_call(inverse_kernel, out_shape=jax.ShapeDtypeStruct((rows, 2 *...  3.44 us

profile of v3, /device:TPU:0, one launch (start us, length us, event | category | flops | bytes accessed | tf_op | source)
XLA Modules:
  0.0 20.1 jit_solution(18221256601952893642)
XLA Ops:
  0.0 0.0 copy-start
  0.0 0.0 copy-start.1
  0.0 0.0 copy-start.2
  0.0 0.0 copy-start.3
  0.0 0.0 copy-start.5
  0.0 0.0 copy-start.6
  0.0 0.0 copy-start.4
  0.0 16.5 %shard_map.127.returned = f32[4,32,256]{2,1,0:T(8,128)S(1)} custom-call(s32[8]{0:T(128)} %offsets_ref.3, f32[128,64,128]{2,1,0:T(8,128)} %bitcast.16, f32[32,128]{1,0:T(8,128)} %bitcast.12, f32[1,128]{1,0:T(1,128)} %bitcast.14, f32[2,512]{1,0:T(2,128)} %phases_ref.1, s32[2,2,512]{2,1,0:T(2,128)} %coverage_ref.1, f32[2,4,128]{2,1,0:T(4,128)} %constant.14.clone.twist_ref, ...), custom_call_target="tpu_custom_call" | custom-call | tf_op jit(solution)/shard_map/pallas_call | solution.py:530
  16.6 0.0 copy-done
  16.6 0.0 copy-done.1
  16.6 0.0 copy-done.2
  16.6 0.0 copy-done.3
  16.6 0.0 copy-done.5
  16.6 0.0 copy-done.6
  16.6 0.0 copy-done.4
  16.6 3.4 %shard_map.128 = f32[16,64,128]{2,1,0:T(8,128)} custom-call(s32[8]{0:T(128)S(1)} %copy-done.5, f32[4,32,256]{2,1,0:T(8,128)S(1)} %shard_map.127.returned, f32[32,128]{1,0:T(8,128)S(1)} %bitcast.13, f32[1,128]{1,0:T(1,128)S(1)} %bitcast.15, f32[256,256]{1,0:T(8,128)S(1)} %copy-done, f32[32,8,256]{2,1,0:T(8,128)S(1)} %copy-done.1, ...), custom_call_target="tpu_custom_call" | custom-call | tf_op jit(solution)/shard_map/pallas_call | solution.py:562
Async XLA Ops:
  0.0 16.6 %copy-start = (f32[256,256]{1,0:T(8,128)S(1)}, f32[256,256]{1,0:T(8,128)}, u32[]{:S(2)}) copy-start(f32[256,256]{1,0:T(8,128)} %constant.19.clone.unit_t_far) | copy-start | bytes 786436
  0.0 16.6 %copy-start.1 = (f32[32,8,256]{2,1,0:T(8,128)S(1)}, f32[32,8,256]{2,1,0:T(8,128)}, u32[]{:S(2)}) copy-start(f32[32,8,256]{2,1,0:T(8,128)} %constant.17.clone.pick_far) | copy-start | bytes 786436
  0.0 16.6 %copy-start.2 = (f32[2,128,128]{2,1,0:T(8,128)S(1)}, f32[2,128,128]{2,1,0:T(8,128)}, u32[]{:S(2)}) copy-start(f32[2,128,128]{2,1,0:T(8,128)} %constant.16.clone.turn_far) | copy-start | bytes 393220
  0.0 16.6 %copy-start.3 = (f32[256,256]{1,0:T(8,128)S(1)}, f32[256,256]{1,0:T(8,128)}, u32[]{:S(2)}) copy-start(f32[256,256]{1,0:T(8,128)} %constant.20.clone.outer_t_far) | copy-start | bytes 786436
  0.0 16.6 %copy-start.5 = (s32[8]{0:T(128)S(1)}, s32[8]{0:T(128)}, u32[]{:S(2)}) copy-start(s32[8]{0:T(128)} %offsets_ref.3) | copy-start | bytes 100
  0.0 16.6 %copy-start.6 = (f32[128]{0:T(128)S(1)}, f32[128]{0:T(128)}, u32[]{:S(2)}) copy-start(f32[128]{0:T(128)} %param.15) | copy-start | bytes 1540
  0.0 16.6 %copy-start.4 = (f32[1,4096]{1,0:T(1,128)S(1)}, f32[1,4096]{1,0:T(1,128)}, u32[]{:S(2)}) copy-start(f32[1,4096]{1,0:T(1,128)} %param.14) | copy-start | bytes 49156

commit v4 on v3

--- a/solution.py
+++ b/solution.py
@@ -55,9 +55,10 @@
 
 
 def mm(left, right, transposed=False):
-    dims = (((1,), (1 if transposed else 0,)), ((), ()))
-    dot = functools.partial(lax.dot_general, dimension_numbers=dims, preferred_element_type=F32)
-    return dot(left[0], right[0]) + (dot(left[0], right[1]) + dot(left[1], right[0]))
+    axis = 1 if transposed else 0
+    one = jnp.concatenate([left[0], left[0], left[1]], axis=1)
+    two = jnp.concatenate([right[0], right[1], right[0]], axis=axis)
+    return lax.dot_general(one, two, (((1,), (axis,)), ((), ())), preferred_element_type=F32)
 
 
 def cos_sin(value):
@@ -229,6 +230,40 @@
         fetches[name] = pltpu.make_async_copy(far, near, table_sem.at[i])
         fetches[name].start()
 
+    def gathers():
+        copies = []
+        for i, (mate_sub, mate_pair) in enumerate(grid_mates):
+            copies.append(
+                pltpu.make_async_remote_copy(
+                    src_ref=coverage_ref,
+                    dst_ref=counts.at[sub, pair],
+                    send_sem=cov_send.at[i],
+                    recv_sem=cov_recv.at[i],
+                    device_id={"sub": mate_sub, "wa": mate_pair},
+                    device_id_type=MESH,
+                )
+            )
+        for d in range(1, pair_count):
+            copies.append(
+                pltpu.make_async_remote_copy(
+                    src_ref=phases_ref,
+                    dst_ref=screens.at[pair],
+                    send_sem=ph_send.at[d - 1],
+                    recv_sem=ph_recv.at[d - 1],
+                    device_id={"wa": lax.rem(pair + d, pair_count)},
+                    device_id_type=MESH,
+                )
+            )
+        return copies
+
+    def greet():
+        pl.semaphore_wait(barrier, len(facet_mates) + len(hops))
+        for copy in gathers():
+            copy.start()
+
+    counts[sub, pair] = coverage_ref[...]
+    screens[pair] = phases_ref[...]
+
     gain[pl.ds(0, low, stride=2), :] = correction_ref[...]
     gain[pl.ds(1, low, stride=2), :] = correction_ref[...]
     first_q, turn_cos, turn_sin, is_first, window_rows = offset_tables(
@@ -246,6 +281,7 @@
     spread = jnp.concatenate(groups, axis=1)
     fetches["outer"].wait()
     mixed = mm(split(outer_ref[...]), split(spread))
+    pl.when(sub != 0)(greet)
     fetches["turn"].wait()
     table_cos, table_sin = turn_ref[0], turn_ref[1]
     turned = []
@@ -260,33 +296,7 @@
     turned = jnp.concatenate(turned, axis=0)
     spectrum = mm(picked, split(turned), transposed=True)
 
-    pl.semaphore_wait(barrier, len(facet_mates) + len(hops))
-    copies = []
-    for i, (mate_sub, mate_pair) in enumerate(grid_mates):
-        copy = pltpu.make_async_remote_copy(
-            src_ref=coverage_ref,
-            dst_ref=counts.at[sub, pair],
-            send_sem=cov_send.at[i],
-            recv_sem=cov_recv.at[i],
-            device_id={"sub": mate_sub, "wa": mate_pair},
-            device_id_type=MESH,
-        )
-        copy.start()
-        copies.append(copy)
-    counts[sub, pair] = coverage_ref[...]
-    for d in range(1, pair_count):
-        copy = pltpu.make_async_remote_copy(
-            src_ref=phases_ref,
-            dst_ref=screens.at[pair],
-            send_sem=ph_send.at[d - 1],
-            recv_sem=ph_recv.at[d - 1],
-            device_id={"wa": lax.rem(pair + d, pair_count)},
-            device_id_type=MESH,
-        )
-        copy.start()
-        copies.append(copy)
-    screens[pair] = phases_ref[...]
-
+    pl.when(sub == 0)(greet)
     for s in range(subs):
         here = slice(s * quads, (s + 1) * quads)
         base = s * 4 * quads
@@ -323,7 +333,7 @@
     fetches["unit_t"].wait()
     unit_t = split(unit_t_ref[...])
 
-    for copy in copies:
+    for copy in gathers():
         copy.wait()
     for owner in range(sub_count):
         for p in range(pair_count):

time: 20.3 us -> 19.6 us (0.966)
  Pallas kernels: 20 us -> 19.3 us
    pallas_call x1, Pallas kernels: 16.5 us -> 16.1 us  [on_device(): pl.pallas_call(functools.partial(kernel, (facet_count, sub_count, pair_co...]
    pallas_call x1, Pallas kernels: 3.44 us -> 3.19 us  [on_device(): pl.pallas_call(inverse_kernel, out_shape=jax.ShapeDtypeStruct((rows, 2 *...]
where the time goes in v4:
time: 19.6 us; the launch traced here: 19.4 us
  Pallas kernels  19.3 us (98%)
    pallas_call x1, Pallas kernels, on_device(): pl.pallas_call(functools.partial(kernel, (facet_count, sub_count, pair_co...  16.1 us
    pallas_call x1, Pallas kernels, on_device(): pl.pallas_call(inverse_kernel, out_shape=jax.ShapeDtypeStruct((rows, 2 *...  3.19 us

profile of v4, /device:TPU:0, one launch (start us, length us, event | category | flops | bytes accessed | tf_op | source)
XLA Modules:
  0.0 19.4 jit_solution(72751181896907068)
XLA Ops:
  0.0 0.0 copy-start
  0.0 0.0 copy-start.1
  0.0 0.0 copy-start.2
  0.0 0.0 copy-start.3
  0.0 0.0 copy-start.5
  0.0 0.0 copy-start.6
  0.0 0.0 copy-start.4
  0.0 16.1 %shard_map.127.returned = f32[4,32,256]{2,1,0:T(8,128)S(1)} custom-call(s32[8]{0:T(128)} %offsets_ref.3, f32[128,64,128]{2,1,0:T(8,128)} %bitcast.16, f32[32,128]{1,0:T(8,128)} %bitcast.12, f32[1,128]{1,0:T(1,128)} %bitcast.14, f32[2,512]{1,0:T(2,128)} %phases_ref.1, s32[2,2,512]{2,1,0:T(2,128)} %coverage_ref.1, f32[2,4,128]{2,1,0:T(4,128)} %constant.14.clone.twist_ref, ...), custom_call_target="tpu_custom_call" | custom-call | tf_op jit(solution)/shard_map/pallas_call | solution.py:540
  16.1 0.0 copy-done
  16.1 0.0 copy-done.1
  16.2 0.0 copy-done.2
  16.2 0.0 copy-done.3
  16.2 0.0 copy-done.5
  16.2 0.0 copy-done.6
  16.2 0.0 copy-done.4
  16.2 3.2 %shard_map.128 = f32[16,64,128]{2,1,0:T(8,128)} custom-call(s32[8]{0:T(128)S(1)} %copy-done.5, f32[4,32,256]{2,1,0:T(8,128)S(1)} %shard_map.127.returned, f32[32,128]{1,0:T(8,128)S(1)} %bitcast.13, f32[1,128]{1,0:T(1,128)S(1)} %bitcast.15, f32[256,256]{1,0:T(8,128)S(1)} %copy-done, f32[32,8,256]{2,1,0:T(8,128)S(1)} %copy-done.1, ...), custom_call_target="tpu_custom_call" | custom-call | tf_op jit(solution)/shard_map/pallas_call | solution.py:572
Async XLA Ops:
  0.0 16.1 %copy-start = (f32[256,256]{1,0:T(8,128)S(1)}, f32[256,256]{1,0:T(8,128)}, u32[]{:S(2)}) copy-start(f32[256,256]{1,0:T(8,128)} %constant.19.clone.unit_t_far) | copy-start | bytes 786436
  0.0 16.1 %copy-start.1 = (f32[32,8,256]{2,1,0:T(8,128)S(1)}, f32[32,8,256]{2,1,0:T(8,128)}, u32[]{:S(2)}) copy-start(f32[32,8,256]{2,1,0:T(8,128)} %constant.17.clone.pick_far) | copy-start | bytes 786436
  0.0 16.2 %copy-start.2 = (f32[2,128,128]{2,1,0:T(8,128)S(1)}, f32[2,128,128]{2,1,0:T(8,128)}, u32[]{:S(2)}) copy-start(f32[2,128,128]{2,1,0:T(8,128)} %constant.16.clone.turn_far) | copy-start | bytes 393220
  0.0 16.2 %copy-start.3 = (f32[256,256]{1,0:T(8,128)S(1)}, f32[256,256]{1,0:T(8,128)}, u32[]{:S(2)}) copy-start(f32[256,256]{1,0:T(8,128)} %constant.20.clone.outer_t_far) | copy-start | bytes 786436
  0.0 16.2 %copy-start.5 = (s32[8]{0:T(128)S(1)}, s32[8]{0:T(128)}, u32[]{:S(2)}) copy-start(s32[8]{0:T(128)} %offsets_ref.3) | copy-start | bytes 100
  0.0 16.2 %copy-start.6 = (f32[128]{0:T(128)S(1)}, f32[128]{0:T(128)}, u32[]{:S(2)}) copy-start(f32[128]{0:T(128)} %param.15) | copy-start | bytes 1540
  0.0 16.2 %copy-start.4 = (f32[1,4096]{1,0:T(1,128)S(1)}, f32[1,4096]{1,0:T(1,128)}, u32[]{:S(2)}) copy-start(f32[1,4096]{1,0:T(1,128)} %param.14) | copy-start | bytes 49156

commit v5 on v4

--- a/solution.py
+++ b/solution.py
@@ -169,6 +169,7 @@
     sent,
     arrived,
     back,
+    ordered,
     counts,
     expanded,
     screens,
@@ -235,7 +236,7 @@
         for i, (mate_sub, mate_pair) in enumerate(grid_mates):
             copies.append(
                 pltpu.make_async_remote_copy(
-                    src_ref=coverage_ref,
+                    src_ref=ordered,
                     dst_ref=counts.at[sub, pair],
                     send_sem=cov_send.at[i],
                     recv_sem=cov_recv.at[i],
@@ -261,7 +262,16 @@
         for copy in gathers():
             copy.start()
 
-    counts[sub, pair] = coverage_ref[...]
+    source = lax.broadcasted_iota(jnp.int32, (total, total), 0)
+    inner = lax.broadcasted_iota(jnp.int32, (1, width), 1) * facet_count
+    wanted = jnp.concatenate([inner + k for k in range(facet_count)], axis=1)
+    chooser = jnp.where(source == wanted, 1.0, 0.0).astype(BF16)
+    own = [coverage_ref[i].astype(F32) for i in range(per_sub)]
+    own = jnp.dot(
+        jnp.concatenate(own, axis=0).astype(BF16), chooser, preferred_element_type=F32
+    )
+    ordered[...] = own * (1.0 / (facet_count * planes))
+    counts[sub, pair] = ordered[...]
     screens[pair] = phases_ref[...]
 
     gain[pl.ds(0, low, stride=2), :] = correction_ref[...]
@@ -272,6 +282,7 @@
     fetches["pick"].wait()
     picked = gather_pick(first_q, pick_ref)
 
+    pl.when((sub != 0) & (sub == sub_count - 1))(greet)
     load.wait()
     gains = gain[...]
     groups = []
@@ -281,7 +292,7 @@
     spread = jnp.concatenate(groups, axis=1)
     fetches["outer"].wait()
     mixed = mm(split(outer_ref[...]), split(spread))
-    pl.when(sub != 0)(greet)
+    pl.when((sub != 0) & (sub != sub_count - 1))(greet)
     fetches["turn"].wait()
     table_cos, table_sin = turn_ref[0], turn_ref[1]
     turned = []
@@ -310,26 +321,31 @@
                 cut[g, here, c * width : (c + 1) * width] = jnp.where(keep, one, two) * win
     fetches["unit"].wait()
     unit = split(unit_ref[...])
-    mixed = mm(split(cut[...].reshape(facet_count * span, 2 * width)), unit)
-    for g in range(facet_count):
-        real = mixed[g * span : (g + 1) * span, :width]
-        imag = mixed[g * span : (g + 1) * span, width:]
-        sent[g, :, :width] = real * turn_cos + imag * turn_sin
-        sent[g, :, width:] = imag * turn_cos - real * turn_sin
+    halves, part = sent.shape[0], sent.shape[2]
     forward = []
-    for i, mate in enumerate(facet_mates):
-        copy = pltpu.make_async_remote_copy(
-            src_ref=sent.at[mate],
-            dst_ref=arrived.at[facet],
-            send_sem=fwd_send.at[i],
-            recv_sem=fwd_recv.at[i],
-            device_id={"facet": mate},
-            device_id_type=MESH,
-        )
-        copy.start()
-        forward.append(copy)
-    arrived[facet] = sent[facet]
-
+    for h in range(halves):
+        rows_h = slice(h * part, (h + 1) * part)
+        mixed = mm(split(cut[:, rows_h].reshape(facet_count * part, 2 * width)), unit)
+        tc, ts = turn_cos[rows_h], turn_sin[rows_h]
+        for g in range(facet_count):
+            real = mixed[g * part : (g + 1) * part, :width]
+            imag = mixed[g * part : (g + 1) * part, width:]
+            sent[h, g, :, :width] = real * tc + imag * ts
+            sent[h, g, :, width:] = imag * tc - real * ts
+        copies = []
+        for i, mate in enumerate(facet_mates):
+            copy = pltpu.make_async_remote_copy(
+                src_ref=sent.at[h, mate],
+                dst_ref=arrived.at[h, facet],
+                send_sem=fwd_send.at[h, i],
+                recv_sem=fwd_recv.at[h, i],
+                device_id={"facet": mate},
+                device_id_type=MESH,
+            )
+            copy.start()
+            copies.append(copy)
+        forward.append(copies)
+        arrived[h, facet] = sent[h, facet]
     fetches["unit_t"].wait()
     unit_t = split(unit_t_ref[...])
 
@@ -340,14 +356,8 @@
             for i in range(per_sub):
                 for j in range(per_wa):
                     at = (p * per_wa + j) * span + (owner * per_sub + i) * quads
-                    row = counts[owner, p, i, j : j + 1].astype(F32)
+                    row = counts[owner, p, i * per_wa + j : i * per_wa + j + 1]
                     expanded[at : at + quads, :] = jnp.broadcast_to(row, (quads, total))
-    source = lax.broadcasted_iota(jnp.int32, (total, total), 0)
-    inner = lax.broadcasted_iota(jnp.int32, (1, width), 1) * facet_count
-    wanted = jnp.concatenate([inner + k for k in range(facet_count)], axis=1)
-    chooser = jnp.where(source == wanted, 1.0, 0.0).astype(BF16)
-    weights = jnp.dot(expanded[...].astype(BF16), chooser, preferred_element_type=F32)
-    weights = weights * (1.0 / (facet_count * planes))
     kernels = []
     for p in range(pair_count):
         screen = screens[p]
@@ -356,58 +366,64 @@
             kernels.append((cos_all[j : j + 1], sin_all[j : j + 1]))
     twist = [(twist_ref[0, k : k + 1], twist_ref[1, k : k + 1]) for k in range(facet_count)]
 
-    for copy in forward:
-        copy.wait()
-    pieces = [[] for _ in range(facet_count)]
-    for w in range(planes):
-        parts = []
+    backward = []
+    for h in range(halves):
+        for copy in forward[h]:
+            copy.wait()
+        pieces = [[] for _ in range(facet_count)]
+        for w in range(planes):
+            parts = []
+            for f in range(facet_count):
+                cols = slice(f * width, (f + 1) * width)
+                kc, ks = kernels[w][0][:, cols], kernels[w][1][:, cols]
+                real, imag = arrived[h, f, :, :width], arrived[h, f, :, width:]
+                parts.append((real * kc - imag * ks, real * ks + imag * kc))
+            for k, (real, imag) in enumerate(radix(parts, -1)):
+                tc, ts = twist[k]
+                pieces[k].append(
+                    jnp.concatenate([real * tc - imag * ts, real * ts + imag * tc], axis=1)
+                )
+        stacked = jnp.concatenate([piece for group in pieces for piece in group], axis=0)
+        grid = mm(split(stacked), unit_t)
+        scale = jnp.concatenate(
+            [
+                expanded[w * span + h * part : w * span + (h + 1) * part, k * width : (k + 1) * width]
+                for k in range(facet_count)
+                for w in range(planes)
+            ],
+            axis=0,
+        )
+        weighted = grid * jnp.concatenate([scale, scale], axis=1)
+        image_side = mm(split(weighted), unit)
+        sums = [None] * facet_count
+        for w in range(planes):
+            parts = []
+            for k in range(facet_count):
+                at = (k * planes + w) * part
+                real = image_side[at : at + part, :width]
+                imag = image_side[at : at + part, width:]
+                tc, ts = twist[k]
+                parts.append((real * tc + imag * ts, imag * tc - real * ts))
+            for f, (real, imag) in enumerate(radix(parts, 1)):
+                cols = slice(f * width, (f + 1) * width)
+                kc, ks = kernels[w][0][:, cols], kernels[w][1][:, cols]
+                term = (real * kc + imag * ks, imag * kc - real * ks)
+                sums[f] = term if w == 0 else (sums[f][0] + term[0], sums[f][1] + term[1])
         for f in range(facet_count):
-            cols = slice(f * width, (f + 1) * width)
-            kc, ks = kernels[w][0][:, cols], kernels[w][1][:, cols]
-            real, imag = arrived[f, :, :width], arrived[f, :, width:]
-            parts.append((real * kc - imag * ks, real * ks + imag * kc))
-        for k, (real, imag) in enumerate(radix(parts, -1)):
-            tc, ts = twist[k]
-            pieces[k].append(
-                jnp.concatenate([real * tc - imag * ts, real * ts + imag * tc], axis=1)
+            back[h, f, :, :width] = sums[f][0]
+            back[h, f, :, width:] = sums[f][1]
+        for i, mate in enumerate(facet_mates):
+            copy = pltpu.make_async_remote_copy(
+                src_ref=back.at[h, mate],
+                dst_ref=returned.at[h, facet],
+                send_sem=bwd_send.at[h, i],
+                recv_sem=bwd_recv.at[h, i],
+                device_id={"facet": mate},
+                device_id_type=MESH,
             )
-    stacked = jnp.concatenate([piece for group in pieces for piece in group], axis=0)
-    grid = mm(split(stacked), unit_t)
-    scale = jnp.concatenate(
-        [weights[:, k * width : (k + 1) * width] for k in range(facet_count)], axis=0
-    )
-    weighted = grid * jnp.concatenate([scale, scale], axis=1)
-    image_side = mm(split(weighted), unit)
-    sums = [None] * facet_count
-    for w in range(planes):
-        parts = []
-        for k in range(facet_count):
-            at = (k * planes + w) * span
-            real = image_side[at : at + span, :width]
-            imag = image_side[at : at + span, width:]
-            tc, ts = twist[k]
-            parts.append((real * tc + imag * ts, imag * tc - real * ts))
-        for f, (real, imag) in enumerate(radix(parts, 1)):
-            cols = slice(f * width, (f + 1) * width)
-            kc, ks = kernels[w][0][:, cols], kernels[w][1][:, cols]
-            term = (real * kc + imag * ks, imag * kc - real * ks)
-            sums[f] = term if w == 0 else (sums[f][0] + term[0], sums[f][1] + term[1])
-    for f in range(facet_count):
-        back[f, :, :width] = sums[f][0]
-        back[f, :, width:] = sums[f][1]
-    backward = []
-    for i, mate in enumerate(facet_mates):
-        copy = pltpu.make_async_remote_copy(
-            src_ref=back.at[mate],
-            dst_ref=returned.at[facet],
-            send_sem=bwd_send.at[i],
-            recv_sem=bwd_recv.at[i],
-            device_id={"facet": mate},
-            device_id_type=MESH,
-        )
-        copy.start()
-        backward.append(copy)
-    returned[facet] = back[facet]
+            copy.start()
+            backward.append(copy)
+        returned[h, facet] = back[h, facet]
     for copy in backward:
         copy.wait()
 
@@ -432,7 +448,8 @@
     table_sem,
     out_sem,
 ):
-    facet_count, span, double = returned.shape
+    halves, facet_count, part, double = returned.shape
+    span = halves * part
     width = double // 2
     subs = offsets_ref.shape[0]
     low = pick_ref.shape[0]
@@ -456,7 +473,8 @@
     )
     unturned = []
     for g in range(facet_count):
-        real, imag = returned[g, :, :width], returned[g, :, width:]
+        whole = jnp.concatenate([returned[h, g] for h in range(halves)], axis=0)
+        real, imag = whole[:, :width], whole[:, width:]
         unturned.append(
             jnp.concatenate(
                 [real * turn_cos - imag * turn_sin, real * turn_sin + imag * turn_cos], axis=1
@@ -533,8 +551,10 @@
     far = pl.BlockSpec(memory_space=pltpu.HBM)
     others = sub_count * pair_count - 1
     dma = pltpu.SemaphoreType.DMA
-    block = (facet_count, span, 2 * width)
+    halves = 2 if subs % 2 == 0 and (span // 2) % 8 == 0 else 1
+    block = (halves, facet_count, span // halves, 2 * width)
     gains = correction.reshape(lines, width)
+    held = coverage.shape[0] * coverage.shape[1]
     window = window.reshape(1, width)
     first_tables = [outer, turn, pick, unit, unit_t]
     returned = pl.pallas_call(
@@ -545,18 +565,19 @@
         scratch_shapes=[
             pltpu.VMEM((rows, 2 * lines, width), F32),
             pltpu.VMEM((2 * lines, width), F32),
+            pltpu.VMEM((facet_count, span, 2 * width), F32),
             pltpu.VMEM(block, F32),
             pltpu.VMEM(block, F32),
             pltpu.VMEM(block, F32),
-            pltpu.VMEM(block, F32),
-            pltpu.VMEM((sub_count, pair_count) + coverage.shape, jnp.int32),
+            pltpu.VMEM((held, total), F32),
+            pltpu.VMEM((sub_count, pair_count, held, total), F32),
             pltpu.VMEM((coverage.shape[1] * pair_count * span, total), F32),
             pltpu.VMEM((pair_count,) + phases.shape, F32),
             dma,
-            dma((facet_count - 1,)),
-            dma((facet_count - 1,)),
-            dma((facet_count - 1,)),
-            dma((facet_count - 1,)),
+            dma((halves, facet_count - 1)),
+            dma((halves, facet_count - 1)),
+            dma((halves, facet_count - 1)),
+            dma((halves, facet_count - 1)),
             dma((others,)),
             dma((others,)),
             dma((max(pair_count - 1, 1),)),

time: 19.6 us -> 18.7 us (0.954)
  Pallas kernels: 19.3 us -> 18.4 us
    pallas_call x1, Pallas kernels: 16.1 us -> 15.2 us  [on_device(): pl.pallas_call(functools.partial(kernel, (facet_count, sub_count, pair_co...]
where the time goes in v5:
time: 18.7 us; the launch traced here: 18.5 us
  Pallas kernels  18.4 us (98%)
    pallas_call x1, Pallas kernels, on_device(): pl.pallas_call(functools.partial(kernel, (facet_count, sub_count, pair_co...  15.2 us
    pallas_call x1, Pallas kernels, on_device(): pl.pallas_call(inverse_kernel, out_shape=jax.ShapeDtypeStruct((rows, 2 *...  3.19 us

profile of v5, /device:TPU:0, one launch (start us, length us, event | category | flops | bytes accessed | tf_op | source)
XLA Modules:
  0.0 18.5 jit_solution(13169255676872285850)
XLA Ops:
  0.0 0.0 copy-start
  0.0 0.0 copy-start.1
  0.0 0.0 copy-start.2
  0.0 0.0 copy-start.3
  0.0 0.0 copy-start.5
  0.0 0.0 copy-start.6
  0.0 0.0 copy-start.4
  0.0 15.2 %shard_map.127.returned = f32[2,4,16,256]{3,2,1,0:T(8,128)S(1)} custom-call(s32[8]{0:T(128)} %offsets_ref.3, f32[128,64,128]{2,1,0:T(8,128)} %bitcast.16, f32[32,128]{1,0:T(8,128)} %bitcast.12, f32[1,128]{1,0:T(1,128)} %bitcast.14, f32[2,512]{1,0:T(2,128)} %phases_ref.1, s32[2,2,512]{2,1,0:T(2,128)} %coverage_ref.1, f32[2,4,128]{2,1,0:T(4,128)} %constant.14.clone.twist_ref, ...), custom_call_target="tpu_custom_call" | custom-call | tf_op jit(solution)/shard_map/pallas_call | solution.py:560
  15.3 0.0 copy-done
  15.3 0.0 copy-done.1
  15.3 0.0 copy-done.2
  15.3 0.0 copy-done.3
  15.3 0.0 copy-done.5
  15.3 0.0 copy-done.6
  15.4 0.0 copy-done.4
  15.4 3.2 %shard_map.128 = f32[16,64,128]{2,1,0:T(8,128)} custom-call(s32[8]{0:T(128)S(1)} %copy-done.5, f32[2,4,16,256]{3,2,1,0:T(8,128)S(1)} %shard_map.127.returned, f32[32,128]{1,0:T(8,128)S(1)} %bitcast.13, f32[1,128]{1,0:T(1,128)S(1)} %bitcast.15, f32[256,256]{1,0:T(8,128)S(1)} %copy-done, f32[32,8,256]{2,1,0:T(8,128)S(1)} %copy-done.1, ...), custom_call_target="tpu_custom_call" | custom-call | tf_op jit(solution)/shard_map/pallas_call | solution.py:593
Async XLA Ops:
  0.0 15.3 %copy-start = (f32[256,256]{1,0:T(8,128)S(1)}, f32[256,256]{1,0:T(8,128)}, u32[]{:S(2)}) copy-start(f32[256,256]{1,0:T(8,128)} %constant.19.clone.unit_t_far) | copy-start | bytes 786436
  0.0 15.3 %copy-start.1 = (f32[32,8,256]{2,1,0:T(8,128)S(1)}, f32[32,8,256]{2,1,0:T(8,128)}, u32[]{:S(2)}) copy-start(f32[32,8,256]{2,1,0:T(8,128)} %constant.17.clone.pick_far) | copy-start | bytes 786436
  0.0 15.3 %copy-start.2 = (f32[2,128,128]{2,1,0:T(8,128)S(1)}, f32[2,128,128]{2,1,0:T(8,128)}, u32[]{:S(2)}) copy-start(f32[2,128,128]{2,1,0:T(8,128)} %constant.16.clone.turn_far) | copy-start | bytes 393220
  0.0 15.3 %copy-start.3 = (f32[256,256]{1,0:T(8,128)S(1)}, f32[256,256]{1,0:T(8,128)}, u32[]{:S(2)}) copy-start(f32[256,256]{1,0:T(8,128)} %constant.20.clone.outer_t_far) | copy-start | bytes 786436
  0.0 15.3 %copy-start.5 = (s32[8]{0:T(128)S(1)}, s32[8]{0:T(128)}, u32[]{:S(2)}) copy-start(s32[8]{0:T(128)} %offsets_ref.3) | copy-start | bytes 100
  0.0 15.3 %copy-start.6 = (f32[128]{0:T(128)S(1)}, f32[128]{0:T(128)}, u32[]{:S(2)}) copy-start(f32[128]{0:T(128)} %param.15) | copy-start | bytes 1540
  0.0 15.3 %copy-start.4 = (f32[1,4096]{1,0:T(1,128)S(1)}, f32[1,4096]{1,0:T(1,128)}, u32[]{:S(2)}) copy-start(f32[1,4096]{1,0:T(1,128)} %param.14) | copy-start | bytes 49156

commit v6 on v5

--- a/solution.py
+++ b/solution.py
@@ -214,10 +214,27 @@
         pl.semaphore_signal(
             barrier, inc=1, device_id={"sub": mate_sub, "wa": mate_pair}, device_id_type=MESH
         )
-    load = pltpu.make_async_copy(
-        facets_ref.at[pl.ds((sub * pair_count + pair) * rows, rows)], image, load_sem
-    )
-    load.start()
+    pair_size = 2 if facet_count % 2 == 0 else 1
+    pairs = facet_count // pair_size
+    order = [lax.rem(facet // pair_size + 1 + step, pairs) for step in range(pairs)]
+    slots = [
+        order[step] * pair_size + lax.rem(facet + g, pair_size)
+        for step in range(pairs - 1)
+        for g in range(pair_size)
+    ]
+    near = order[-1] * pair_size
+    far_first = slots + [near + lax.rem(facet + 1 + g, pair_size) for g in range(pair_size - 1)]
+    batch = pair_size * quads
+    first_row = (sub * pair_count + pair) * rows
+    loads = []
+    for step, which in enumerate(order):
+        load = pltpu.make_async_copy(
+            facets_ref.at[pl.ds(first_row + which * batch, batch)],
+            image.at[pl.ds(step * batch, batch)],
+            load_sem.at[step],
+        )
+        load.start()
+        loads.append(load)
     fetches = {}
     for i, (name, far, near) in enumerate(
         (
@@ -283,69 +300,78 @@
     picked = gather_pick(first_q, pick_ref)
 
     pl.when((sub != 0) & (sub == sub_count - 1))(greet)
-    load.wait()
     gains = gain[...]
-    groups = []
-    for g in range(facet_count):
-        blocks = [image[g * quads + i] * gains for i in range(quads)]
-        groups.append(jnp.concatenate(swap_blocks(blocks, low), axis=0))
-    spread = jnp.concatenate(groups, axis=1)
     fetches["outer"].wait()
-    mixed = mm(split(outer_ref[...]), split(spread))
-    pl.when((sub != 0) & (sub != sub_count - 1))(greet)
+    outer = split(outer_ref[...])
     fetches["turn"].wait()
     table_cos, table_sin = turn_ref[0], turn_ref[1]
-    turned = []
-    for g in range(facet_count):
-        real = mixed[:width, g * width : (g + 1) * width]
-        imag = mixed[width:, g * width : (g + 1) * width]
-        turned.append(
-            jnp.concatenate(
-                [real * table_cos - imag * table_sin, real * table_sin + imag * table_cos], axis=1
-            )
-        )
-    turned = jnp.concatenate(turned, axis=0)
-    spectrum = mm(picked, split(turned), transposed=True)
-
-    pl.when(sub == 0)(greet)
-    for s in range(subs):
-        here = slice(s * quads, (s + 1) * quads)
-        base = s * 4 * quads
-        keep = is_first[here]
-        win = window_rows[here]
-        for g in range(facet_count):
-            cols = slice(g * width, (g + 1) * width)
-            for c in range(2):
-                one = spectrum[base + c * quads : base + (c + 1) * quads, cols]
-                two = spectrum[base + (2 + c) * quads : base + (3 + c) * quads, cols]
-                cut[g, here, c * width : (c + 1) * width] = jnp.where(keep, one, two) * win
     fetches["unit"].wait()
     unit = split(unit_ref[...])
-    halves, part = sent.shape[0], sent.shape[2]
     forward = []
-    for h in range(halves):
-        rows_h = slice(h * part, (h + 1) * part)
-        mixed = mm(split(cut[:, rows_h].reshape(facet_count * part, 2 * width)), unit)
-        tc, ts = turn_cos[rows_h], turn_sin[rows_h]
-        for g in range(facet_count):
-            real = mixed[g * part : (g + 1) * part, :width]
-            imag = mixed[g * part : (g + 1) * part, width:]
-            sent[h, g, :, :width] = real * tc + imag * ts
-            sent[h, g, :, width:] = imag * tc - real * ts
-        copies = []
-        for i, mate in enumerate(facet_mates):
+    for step in range(pairs):
+        loads[step].wait()
+        groups = []
+        for g in range(pair_size):
+            at = step * batch + g * quads
+            blocks = [image[at + i] * gains for i in range(quads)]
+            groups.append(jnp.concatenate(swap_blocks(blocks, low), axis=0))
+        spread = jnp.concatenate(groups, axis=1)
+        mixed = mm(outer, split(spread))
+        turned = []
+        for g in range(pair_size):
+            real = mixed[:width, g * width : (g + 1) * width]
+            imag = mixed[width:, g * width : (g + 1) * width]
+            turned.append(
+                jnp.concatenate(
+                    [real * table_cos - imag * table_sin, real * table_sin + imag * table_cos],
+                    axis=1,
+                )
+            )
+        turned = jnp.concatenate(turned, axis=0)
+        spectrum = mm(picked, split(turned), transposed=True)
+        if step == 0:
+            pl.when((sub != 0) & (sub != sub_count - 1))(greet)
+        for s in range(subs):
+            here = slice(s * quads, (s + 1) * quads)
+            base = s * 4 * quads
+            keep = is_first[here]
+            win = window_rows[here]
+            for g in range(pair_size):
+                cols = slice(g * width, (g + 1) * width)
+                for c in range(2):
+                    one = spectrum[base + c * quads : base + (c + 1) * quads, cols]
+                    two = spectrum[base + (2 + c) * quads : base + (3 + c) * quads, cols]
+                    cut[step, g, here, c * width : (c + 1) * width] = (
+                        jnp.where(keep, one, two) * win
+                    )
+        mixed = mm(split(cut[step].reshape(pair_size * span, 2 * width)), unit)
+        for g in range(pair_size):
+            real = mixed[g * span : (g + 1) * span, :width]
+            imag = mixed[g * span : (g + 1) * span, width:]
+            sent[step, g, :, :width] = real * turn_cos + imag * turn_sin
+            sent[step, g, :, width:] = imag * turn_cos - real * turn_sin
+        if step == 0:
+            pl.when(sub == 0)(greet)
+        for g in range(pair_size):
+            if step < pairs - 1:
+                slot = lax.rem(facet + g, pair_size)
+                mate = order[step] * pair_size + slot
+            elif g < pair_size - 1:
+                slot = lax.rem(facet + 1 + g, pair_size)
+                mate = order[step] * pair_size + slot
+            else:
+                continue
             copy = pltpu.make_async_remote_copy(
-                src_ref=sent.at[h, mate],
-                dst_ref=arrived.at[h, facet],
-                send_sem=fwd_send.at[h, i],
-                recv_sem=fwd_recv.at[h, i],
+                src_ref=sent.at[step, slot],
+                dst_ref=arrived.at[facet],
+                send_sem=fwd_send.at[step * pair_size + g],
+                recv_sem=fwd_recv.at[step * pair_size + g],
                 device_id={"facet": mate},
                 device_id_type=MESH,
             )
             copy.start()
-            copies.append(copy)
-        forward.append(copies)
-        arrived[h, facet] = sent[h, facet]
+            forward.append(copy)
+    arrived[facet] = sent[pairs - 1, lax.rem(facet, pair_size)]
     fetches["unit_t"].wait()
     unit_t = split(unit_t_ref[...])
 
@@ -367,16 +393,18 @@
     twist = [(twist_ref[0, k : k + 1], twist_ref[1, k : k + 1]) for k in range(facet_count)]
 
     backward = []
+    halves, part = back.shape[0], back.shape[2]
+    for copy in forward:
+        copy.wait()
     for h in range(halves):
-        for copy in forward[h]:
-            copy.wait()
         pieces = [[] for _ in range(facet_count)]
         for w in range(planes):
             parts = []
             for f in range(facet_count):
                 cols = slice(f * width, (f + 1) * width)
                 kc, ks = kernels[w][0][:, cols], kernels[w][1][:, cols]
-                real, imag = arrived[h, f, :, :width], arrived[h, f, :, width:]
+                both = arrived[f, h * part : (h + 1) * part, :]
+                real, imag = both[:, :width], both[:, width:]
                 parts.append((real * kc - imag * ks, real * ks + imag * kc))
             for k, (real, imag) in enumerate(radix(parts, -1)):
                 tc, ts = twist[k]
@@ -412,7 +440,7 @@
         for f in range(facet_count):
             back[h, f, :, :width] = sums[f][0]
             back[h, f, :, width:] = sums[f][1]
-        for i, mate in enumerate(facet_mates):
+        for i, mate in enumerate(far_first):
             copy = pltpu.make_async_remote_copy(
                 src_ref=back.at[h, mate],
                 dst_ref=returned.at[h, facet],
@@ -433,19 +461,14 @@
     returned,
     correction_ref,
     window_ref,
-    unit_t_far,
-    pick_far,
-    turn_far,
-    outer_t_far,
+    unit_t_ref,
+    pick_ref,
+    turn_ref,
+    outer_t_ref,
     out_ref,
     gain,
     segments,
     image,
-    unit_t_ref,
-    pick_ref,
-    turn_ref,
-    outer_t_ref,
-    table_sem,
     out_sem,
 ):
     halves, facet_count, part, double = returned.shape
@@ -454,17 +477,6 @@
     subs = offsets_ref.shape[0]
     low = pick_ref.shape[0]
     quads = width // low
-    fetches = {}
-    for i, (name, far, near) in enumerate(
-        (
-            ("unit_t", unit_t_far, unit_t_ref),
-            ("pick", pick_far, pick_ref),
-            ("turn", turn_far, turn_ref),
-            ("outer_t", outer_t_far, outer_t_ref),
-        )
-    ):
-        fetches[name] = pltpu.make_async_copy(far, near, table_sem.at[i])
-        fetches[name].start()
     gain[pl.ds(0, low, stride=2), :] = correction_ref[...]
     gain[pl.ds(1, low, stride=2), :] = correction_ref[...]
     gains = gain[...]
@@ -481,7 +493,6 @@
             )
         )
     unturned = jnp.concatenate(unturned, axis=0)
-    fetches["unit_t"].wait()
     mixed = mm(split(unturned), split(unit_t_ref[...]))
     win_first = jnp.where(is_first, window_rows, 0.0)
     win_second = jnp.where(is_first, 0.0, window_rows)
@@ -494,36 +505,40 @@
                 for s in range(subs):
                     at = (4 * s + 2 * h + c) * quads
                     segments[at : at + quads, cols] = masked[s * quads : (s + 1) * quads]
-    columns = jnp.concatenate(
-        [segments[:, g * width : (g + 1) * width].T for g in range(facet_count)], axis=0
-    )
-    fetches["pick"].wait()
-    fine = mm(split(columns), gather_pick(first_q, pick_ref))
-    fetches["turn"].wait()
+    picked = gather_pick(first_q, pick_ref)
     table_cos, table_sin = turn_ref[0], turn_ref[1]
-    reals, imags = [], []
-    for g in range(facet_count):
-        real = fine[g * width : (g + 1) * width, :width]
-        imag = fine[g * width : (g + 1) * width, width:]
-        reals.append(real * table_cos + imag * table_sin)
-        imags.append(imag * table_cos - real * table_sin)
-    joined = jnp.concatenate(
-        [jnp.concatenate(reals, axis=1), jnp.concatenate(imags, axis=1)], axis=0
-    )
-    fetches["outer_t"].wait()
-    spread = mm(split(outer_t_ref[...]), split(joined))
-    part = 2 * width // quads
+    outer_t = split(outer_t_ref[...])
+    share = 2 * width // quads
+    pair_size = 2 if facet_count % 2 == 0 else 1
     stores = []
-    for g in range(facet_count):
-        cols = slice(g * width, (g + 1) * width)
-        blocks = [spread[i * part : (i + 1) * part, cols] for i in range(quads)]
-        for i, block in enumerate(swap_blocks(blocks, low)):
-            image[g * quads + i] = block * gains
-        store = pltpu.make_async_copy(
-            image.at[pl.ds(g * quads, quads)], out_ref.at[pl.ds(g * quads, quads)], out_sem.at[g]
+    for first in range(0, facet_count, pair_size):
+        here = range(first, first + pair_size)
+        columns = jnp.concatenate(
+            [segments[:, g * width : (g + 1) * width].T for g in here], axis=0
         )
-        store.start()
-        stores.append(store)
+        fine = mm(split(columns), picked)
+        reals, imags = [], []
+        for g in range(pair_size):
+            real = fine[g * width : (g + 1) * width, :width]
+            imag = fine[g * width : (g + 1) * width, width:]
+            reals.append(real * table_cos + imag * table_sin)
+            imags.append(imag * table_cos - real * table_sin)
+        joined = jnp.concatenate(
+            [jnp.concatenate(reals, axis=1), jnp.concatenate(imags, axis=1)], axis=0
+        )
+        spread = mm(outer_t, split(joined))
+        for j, g in enumerate(here):
+            cols = slice(j * width, (j + 1) * width)
+            blocks = [spread[i * share : (i + 1) * share, cols] for i in range(quads)]
+            for i, block in enumerate(swap_blocks(blocks, low)):
+                image[g * quads + i] = block * gains
+            store = pltpu.make_async_copy(
+                image.at[pl.ds(g * quads, quads)],
+                out_ref.at[pl.ds(g * quads, quads)],
+                out_sem.at[g],
+            )
+            store.start()
+            stores.append(store)
     for store in stores:
         store.wait()
 
@@ -554,6 +569,7 @@
     halves = 2 if subs % 2 == 0 and (span // 2) % 8 == 0 else 1
     block = (halves, facet_count, span // halves, 2 * width)
     gains = correction.reshape(lines, width)
+    pair_size = 2 if facet_count % 2 == 0 else 1
     held = coverage.shape[0] * coverage.shape[1]
     window = window.reshape(1, width)
     first_tables = [outer, turn, pick, unit, unit_t]
@@ -565,17 +581,17 @@
         scratch_shapes=[
             pltpu.VMEM((rows, 2 * lines, width), F32),
             pltpu.VMEM((2 * lines, width), F32),
+            pltpu.VMEM((facet_count // pair_size, pair_size, span, 2 * width), F32),
+            pltpu.VMEM((facet_count // pair_size, pair_size, span, 2 * width), F32),
             pltpu.VMEM((facet_count, span, 2 * width), F32),
-            pltpu.VMEM(block, F32),
-            pltpu.VMEM(block, F32),
             pltpu.VMEM(block, F32),
             pltpu.VMEM((held, total), F32),
             pltpu.VMEM((sub_count, pair_count, held, total), F32),
             pltpu.VMEM((coverage.shape[1] * pair_count * span, total), F32),
             pltpu.VMEM((pair_count,) + phases.shape, F32),
-            dma,
-            dma((halves, facet_count - 1)),
-            dma((halves, facet_count - 1)),
+            dma((facet_count // pair_size,)),
+            dma((facet_count - 1,)),
+            dma((facet_count - 1,)),
             dma((halves, facet_count - 1)),
             dma((halves, facet_count - 1)),
             dma((others,)),
@@ -593,15 +609,14 @@
     result = pl.pallas_call(
         inverse_kernel,
         out_shape=jax.ShapeDtypeStruct((rows, 2 * lines, width), F32),
-        in_specs=[smem] + [vmem] * 3 + [pl.BlockSpec(memory_space=pl.ANY)] * len(second_tables),
+        in_specs=[smem] + [vmem] * (3 + len(second_tables)),
         out_specs=far,
         scratch_shapes=[
             pltpu.VMEM((2 * lines, width), F32),
             pltpu.VMEM((4 * span, total), F32),
             pltpu.VMEM((rows, 2 * lines, width), F32),
-        ]
-        + [pltpu.VMEM(table.shape, F32) for table in second_tables]
-        + [dma((len(second_tables),)), dma((facet_count,))],
+            dma((facet_count,)),
+        ],
         compiler_params=pltpu.CompilerParams(vmem_limit_bytes=48 * 1024 * 1024),
     )(offsets, returned, gains, window, *map(jnp.asarray, second_tables))
     result = jnp.transpose(result.reshape(rows, lines, 2, width), (0, 2, 1, 3))

time: 18.7 us -> 18.1 us (0.968)
  Pallas kernels: 18.4 us -> 17.8 us
    pallas_call x1, Pallas kernels: 3.19 us -> 2.65 us  [on_device(): pl.pallas_call(inverse_kernel, out_shape=jax.ShapeDtypeStruct((rows, 2 *...]
where the time goes in v6:
time: 18.1 us; the launch traced here: 18 us
  Pallas kernels  17.8 us (98%)
    pallas_call x1, Pallas kernels, on_device(): pl.pallas_call(functools.partial(kernel, (facet_count, sub_count, pair_co...  15.2 us
    pallas_call x1, Pallas kernels, on_device(): pl.pallas_call(inverse_kernel, out_shape=jax.ShapeDtypeStruct((rows, 2 *...  2.65 us

profile of v6, /device:TPU:0, one launch (start us, length us, event | category | flops | bytes accessed | tf_op | source)
XLA Modules:
  0.0 18.0 jit_solution(10019287332028689131)
XLA Ops:
  0.0 0.0 copy-start
  0.0 0.0 copy-start.1
  0.0 0.0 copy-start.2
  0.0 0.0 copy-start.3
  0.0 0.0 copy-start.5
  0.0 0.0 copy-start.6
  0.0 0.0 copy-start.4
  0.0 15.2 %shard_map.127.returned = f32[2,4,16,256]{3,2,1,0:T(8,128)S(1)} custom-call(s32[8]{0:T(128)} %offsets_ref.3, f32[128,64,128]{2,1,0:T(8,128)} %bitcast.16, f32[32,128]{1,0:T(8,128)} %bitcast.12, f32[1,128]{1,0:T(1,128)} %bitcast.14, f32[2,512]{1,0:T(2,128)} %phases_ref.1, s32[2,2,512]{2,1,0:T(2,128)} %coverage_ref.1, f32[2,4,128]{2,1,0:T(4,128)} %constant.14.clone.twist_ref, ...), custom_call_target="tpu_custom_call" | custom-call | tf_op jit(solution)/shard_map/pallas_call | solution.py:576
  15.2 0.0 copy-done
  15.2 0.0 copy-done.1
  15.3 0.0 copy-done.2
  15.3 0.0 copy-done.3
  15.3 0.0 copy-done.5
  15.3 0.0 copy-done.6
  15.3 0.0 copy-done.4
  15.3 2.6 %shard_map.128 = f32[16,64,128]{2,1,0:T(8,128)} custom-call(s32[8]{0:T(128)S(1)} %copy-done.5, f32[2,4,16,256]{3,2,1,0:T(8,128)S(1)} %shard_map.127.returned, f32[32,128]{1,0:T(8,128)S(1)} %bitcast.13, f32[1,128]{1,0:T(1,128)S(1)} %bitcast.15, f32[256,256]{1,0:T(8,128)S(1)} %copy-done, f32[32,8,256]{2,1,0:T(8,128)S(1)} %copy-done.1, ...), custom_call_target="tpu_custom_call" | custom-call | tf_op jit(solution)/shard_map/pallas_call | solution.py:609
Async XLA Ops:
  0.0 15.2 %copy-start = (f32[256,256]{1,0:T(8,128)S(1)}, f32[256,256]{1,0:T(8,128)}, u32[]{:S(2)}) copy-start(f32[256,256]{1,0:T(8,128)} %constant.19.clone.unit_t_far.unit_t_ref) | copy-start | bytes 786436
  0.0 15.2 %copy-start.1 = (f32[32,8,256]{2,1,0:T(8,128)S(1)}, f32[32,8,256]{2,1,0:T(8,128)}, u32[]{:S(2)}) copy-start(f32[32,8,256]{2,1,0:T(8,128)} %constant.17.clone.pick_far.pick_ref) | copy-start | bytes 786436
  0.0 15.3 %copy-start.2 = (f32[2,128,128]{2,1,0:T(8,128)S(1)}, f32[2,128,128]{2,1,0:T(8,128)}, u32[]{:S(2)}) copy-start(f32[2,128,128]{2,1,0:T(8,128)} %constant.16.clone.turn_far.turn_ref) | copy-start | bytes 393220
  0.0 15.3 %copy-start.3 = (f32[256,256]{1,0:T(8,128)S(1)}, f32[256,256]{1,0:T(8,128)}, u32[]{:S(2)}) copy-start(f32[256,256]{1,0:T(8,128)} %constant.20.clone.outer_t_ref) | copy-start | bytes 786436
  0.0 15.3 %copy-start.5 = (s32[8]{0:T(128)S(1)}, s32[8]{0:T(128)}, u32[]{:S(2)}) copy-start(s32[8]{0:T(128)} %offsets_ref.3) | copy-start | bytes 100
  0.0 15.3 %copy-start.6 = (f32[128]{0:T(128)S(1)}, f32[128]{0:T(128)}, u32[]{:S(2)}) copy-start(f32[128]{0:T(128)} %param.15) | copy-start | bytes 1540
  0.0 15.3 %copy-start.4 = (f32[1,4096]{1,0:T(1,128)S(1)}, f32[1,4096]{1,0:T(1,128)}, u32[]{:S(2)}) copy-start(f32[1,4096]{1,0:T(1,128)} %param.14) | copy-start | bytes 49156

commit v7 on v6

--- a/solution.py
+++ b/solution.py
@@ -279,17 +279,22 @@
         for copy in gathers():
             copy.start()
 
-    source = lax.broadcasted_iota(jnp.int32, (total, total), 0)
-    inner = lax.broadcasted_iota(jnp.int32, (1, width), 1) * facet_count
-    wanted = jnp.concatenate([inner + k for k in range(facet_count)], axis=1)
+    source = lax.broadcasted_iota(jnp.int32, (width, width), 0)
+    target = lax.broadcasted_iota(jnp.int32, (1, width), 1)
+    fold = width // facet_count
+    wanted = (target & (fold - 1)) * facet_count + target // fold
     chooser = jnp.where(source == wanted, 1.0, 0.0).astype(BF16)
-    own = [coverage_ref[i].astype(F32) for i in range(per_sub)]
-    own = jnp.dot(
-        jnp.concatenate(own, axis=0).astype(BF16), chooser, preferred_element_type=F32
-    )
-    ordered[...] = own * (1.0 / (facet_count * planes))
+    own = jnp.concatenate([coverage_ref[i].astype(F32) for i in range(per_sub)], axis=0)
+    held = per_sub * per_wa
+    own = jnp.concatenate([own[:, k * width : (k + 1) * width] for k in range(facet_count)], axis=0)
+    own = jnp.dot(own.astype(BF16), chooser, preferred_element_type=F32)
+    own = own * (1.0 / (facet_count * planes))
+    own = [own[k * held : (k + 1) * held] for k in range(facet_count)]
+    for k, block in enumerate(swap_blocks(own, fold)):
+        ordered[:, k * width : (k + 1) * width] = block
     counts[sub, pair] = ordered[...]
     screens[pair] = phases_ref[...]
+    pl.when((sub != 0) & (sub == sub_count - 1))(greet)
 
     gain[pl.ds(0, low, stride=2), :] = correction_ref[...]
     gain[pl.ds(1, low, stride=2), :] = correction_ref[...]
@@ -299,7 +304,6 @@
     fetches["pick"].wait()
     picked = gather_pick(first_q, pick_ref)
 
-    pl.when((sub != 0) & (sub == sub_count - 1))(greet)
     gains = gain[...]
     fetches["outer"].wait()
     outer = split(outer_ref[...])
@@ -317,6 +321,8 @@
             groups.append(jnp.concatenate(swap_blocks(blocks, low), axis=0))
         spread = jnp.concatenate(groups, axis=1)
         mixed = mm(outer, split(spread))
+        if step == 0:
+            pl.when((sub != 0) & (sub != sub_count - 1))(greet)
         turned = []
         for g in range(pair_size):
             real = mixed[:width, g * width : (g + 1) * width]
@@ -329,8 +335,6 @@
             )
         turned = jnp.concatenate(turned, axis=0)
         spectrum = mm(picked, split(turned), transposed=True)
-        if step == 0:
-            pl.when((sub != 0) & (sub != sub_count - 1))(greet)
         for s in range(subs):
             here = slice(s * quads, (s + 1) * quads)
             base = s * 4 * quads
@@ -375,15 +379,9 @@
     fetches["unit_t"].wait()
     unit_t = split(unit_t_ref[...])
 
-    for copy in gathers():
+    arrivals = gathers()
+    for copy in arrivals[len(hops) :]:
         copy.wait()
-    for owner in range(sub_count):
-        for p in range(pair_count):
-            for i in range(per_sub):
-                for j in range(per_wa):
-                    at = (p * per_wa + j) * span + (owner * per_sub + i) * quads
-                    row = counts[owner, p, i * per_wa + j : i * per_wa + j + 1]
-                    expanded[at : at + quads, :] = jnp.broadcast_to(row, (quads, total))
     kernels = []
     for p in range(pair_count):
         screen = screens[p]
@@ -413,6 +411,16 @@
                 )
         stacked = jnp.concatenate([piece for group in pieces for piece in group], axis=0)
         grid = mm(split(stacked), unit_t)
+        if h == 0:
+            for copy in arrivals[: len(hops)]:
+                copy.wait()
+            for owner in range(sub_count):
+                for p in range(pair_count):
+                    for i in range(per_sub):
+                        for j in range(per_wa):
+                            at = (p * per_wa + j) * span + (owner * per_sub + i) * quads
+                            row = counts[owner, p, i * per_wa + j : i * per_wa + j + 1]
+                            expanded[at : at + quads, :] = jnp.broadcast_to(row, (quads, total))
         scale = jnp.concatenate(
             [
                 expanded[w * span + h * part : w * span + (h + 1) * part, k * width : (k + 1) * width]

time: 18.1 us -> 17.5 us (0.967)
  Pallas kernels: 17.8 us -> 17.2 us
    pallas_call x1, Pallas kernels: 15.2 us -> 14.5 us  [on_device(): pl.pallas_call(functools.partial(kernel, (facet_count, sub_count, pair_co...]
where the time goes in v7:
time: 17.5 us; the launch traced here: 17.3 us
  Pallas kernels  17.2 us (98%)
    pallas_call x1, Pallas kernels, on_device(): pl.pallas_call(functools.partial(kernel, (facet_count, sub_count, pair_co...  14.5 us
    pallas_call x1, Pallas kernels, on_device(): pl.pallas_call(inverse_kernel, out_shape=jax.ShapeDtypeStruct((rows, 2 *...  2.65 us

profile of v7, /device:TPU:0, one launch (start us, length us, event | category | flops | bytes accessed | tf_op | source)
XLA Modules:
  0.0 17.3 jit_solution(17088126048999412903)
XLA Ops:
  0.0 0.0 copy-start
  0.0 0.0 copy-start.1
  0.0 0.0 copy-start.2
  0.0 0.0 copy-start.3
  0.0 0.0 copy-start.5
  0.0 0.0 copy-start.6
  0.0 0.0 copy-start.4
  0.0 14.5 %shard_map.127.returned = f32[2,4,16,256]{3,2,1,0:T(8,128)S(1)} custom-call(s32[8]{0:T(128)} %offsets_ref.3, f32[128,64,128]{2,1,0:T(8,128)} %bitcast.16, f32[32,128]{1,0:T(8,128)} %bitcast.12, f32[1,128]{1,0:T(1,128)} %bitcast.14, f32[2,512]{1,0:T(2,128)} %phases_ref.1, s32[2,2,512]{2,1,0:T(2,128)} %coverage_ref.1, f32[2,4,128]{2,1,0:T(4,128)} %constant.14.clone.twist_ref, ...), custom_call_target="tpu_custom_call" | custom-call | tf_op jit(solution)/shard_map/pallas_call | solution.py:584
  14.6 0.0 copy-done
  14.6 0.0 copy-done.1
  14.6 0.0 copy-done.2
  14.6 0.0 copy-done.3
  14.6 0.0 copy-done.5
  14.6 0.0 copy-done.6
  14.6 0.0 copy-done.4
  14.6 2.6 %shard_map.128 = f32[16,64,128]{2,1,0:T(8,128)} custom-call(s32[8]{0:T(128)S(1)} %copy-done.5, f32[2,4,16,256]{3,2,1,0:T(8,128)S(1)} %shard_map.127.returned, f32[32,128]{1,0:T(8,128)S(1)} %bitcast.13, f32[1,128]{1,0:T(1,128)S(1)} %bitcast.15, f32[256,256]{1,0:T(8,128)S(1)} %copy-done, f32[32,8,256]{2,1,0:T(8,128)S(1)} %copy-done.1, ...), custom_call_target="tpu_custom_call" | custom-call | tf_op jit(solution)/shard_map/pallas_call | solution.py:617
Async XLA Ops:
  0.0 14.6 %copy-start = (f32[256,256]{1,0:T(8,128)S(1)}, f32[256,256]{1,0:T(8,128)}, u32[]{:S(2)}) copy-start(f32[256,256]{1,0:T(8,128)} %constant.19.clone.unit_t_far.unit_t_ref) | copy-start | bytes 786436
  0.0 14.6 %copy-start.1 = (f32[32,8,256]{2,1,0:T(8,128)S(1)}, f32[32,8,256]{2,1,0:T(8,128)}, u32[]{:S(2)}) copy-start(f32[32,8,256]{2,1,0:T(8,128)} %constant.17.clone.pick_far.pick_ref) | copy-start | bytes 786436
  0.0 14.6 %copy-start.2 = (f32[2,128,128]{2,1,0:T(8,128)S(1)}, f32[2,128,128]{2,1,0:T(8,128)}, u32[]{:S(2)}) copy-start(f32[2,128,128]{2,1,0:T(8,128)} %constant.16.clone.turn_far.turn_ref) | copy-start | bytes 393220
  0.0 14.6 %copy-start.3 = (f32[256,256]{1,0:T(8,128)S(1)}, f32[256,256]{1,0:T(8,128)}, u32[]{:S(2)}) copy-start(f32[256,256]{1,0:T(8,128)} %constant.20.clone.outer_t_ref) | copy-start | bytes 786436
  0.0 14.6 %copy-start.5 = (s32[8]{0:T(128)S(1)}, s32[8]{0:T(128)}, u32[]{:S(2)}) copy-start(s32[8]{0:T(128)} %offsets_ref.3) | copy-start | bytes 100
  0.0 14.6 %copy-start.6 = (f32[128]{0:T(128)S(1)}, f32[128]{0:T(128)}, u32[]{:S(2)}) copy-start(f32[128]{0:T(128)} %param.15) | copy-start | bytes 1540
  0.0 14.6 %copy-start.4 = (f32[1,4096]{1,0:T(1,128)S(1)}, f32[1,4096]{1,0:T(1,128)}, u32[]{:S(2)}) copy-start(f32[1,4096]{1,0:T(1,128)} %param.14) | copy-start | bytes 49156

commit v8 on v7

--- a/solution.py
+++ b/solution.py
@@ -152,11 +152,11 @@
     geometry,
     offsets_ref,
     facets_ref,
-    correction_ref,
-    window_ref,
-    phases_ref,
-    coverage_ref,
-    twist_ref,
+    correction_far,
+    window_far,
+    phases_far,
+    coverage_far,
+    twist_far,
     outer_far,
     turn_far,
     pick_far,
@@ -188,6 +188,12 @@
     unit_ref,
     unit_t_ref,
     table_sem,
+    correction_ref,
+    window_ref,
+    phases_ref,
+    coverage_ref,
+    twist_ref,
+    small_sem,
 ):
     facet_count, sub_count, pair_count = geometry
     facet = lax.axis_index("facet")
@@ -214,6 +220,18 @@
         pl.semaphore_signal(
             barrier, inc=1, device_id={"sub": mate_sub, "wa": mate_pair}, device_id_type=MESH
         )
+    fetches = {}
+    for i, (name, far, near) in enumerate(
+        (
+            ("coverage", coverage_far, coverage_ref),
+            ("phases", phases_far, phases_ref),
+            ("correction", correction_far, correction_ref),
+            ("window", window_far, window_ref),
+            ("twist", twist_far, twist_ref),
+        )
+    ):
+        fetches[name] = pltpu.make_async_copy(far, near, small_sem.at[i])
+        fetches[name].start()
     pair_size = 2 if facet_count % 2 == 0 else 1
     pairs = facet_count // pair_size
     order = [lax.rem(facet // pair_size + 1 + step, pairs) for step in range(pairs)]
@@ -235,7 +253,6 @@
         )
         load.start()
         loads.append(load)
-    fetches = {}
     for i, (name, far, near) in enumerate(
         (
             ("outer", outer_far, outer_ref),
@@ -284,6 +301,7 @@
     fold = width // facet_count
     wanted = (target & (fold - 1)) * facet_count + target // fold
     chooser = jnp.where(source == wanted, 1.0, 0.0).astype(BF16)
+    fetches["coverage"].wait()
     own = jnp.concatenate([coverage_ref[i].astype(F32) for i in range(per_sub)], axis=0)
     held = per_sub * per_wa
     own = jnp.concatenate([own[:, k * width : (k + 1) * width] for k in range(facet_count)], axis=0)
@@ -293,17 +311,20 @@
     for k, block in enumerate(swap_blocks(own, fold)):
         ordered[:, k * width : (k + 1) * width] = block
     counts[sub, pair] = ordered[...]
+    fetches["phases"].wait()
     screens[pair] = phases_ref[...]
     pl.when((sub != 0) & (sub == sub_count - 1))(greet)
 
-    gain[pl.ds(0, low, stride=2), :] = correction_ref[...]
-    gain[pl.ds(1, low, stride=2), :] = correction_ref[...]
+    fetches["window"].wait()
     first_q, turn_cos, turn_sin, is_first, window_rows = offset_tables(
         offsets_ref, window_ref, quads
     )
     fetches["pick"].wait()
     picked = gather_pick(first_q, pick_ref)
 
+    fetches["correction"].wait()
+    gain[pl.ds(0, low, stride=2), :] = correction_ref[...]
+    gain[pl.ds(1, low, stride=2), :] = correction_ref[...]
     gains = gain[...]
     fetches["outer"].wait()
     outer = split(outer_ref[...])
@@ -388,6 +409,7 @@
         cos_all, sin_all = cos_sin(screen)
         for j in range(per_wa):
             kernels.append((cos_all[j : j + 1], sin_all[j : j + 1]))
+    fetches["twist"].wait()
     twist = [(twist_ref[0, k : k + 1], twist_ref[1, k : k + 1]) for k in range(facet_count)]
 
     backward = []
@@ -584,7 +606,7 @@
     returned = pl.pallas_call(
         functools.partial(kernel, (facet_count, sub_count, pair_count)),
         out_shape=pltpu.VMEM(block, F32),
-        in_specs=[smem, far] + [vmem] * 5 + [far] * len(first_tables),
+        in_specs=[smem] + [far] * (6 + len(first_tables)),
         out_specs=vmem,
         scratch_shapes=[
             pltpu.VMEM((rows, 2 * lines, width), F32),
@@ -608,7 +630,15 @@
             dma((max(pair_count - 1, 1),)),
         ]
         + [pltpu.VMEM(table.shape, F32) for table in first_tables]
-        + [dma((len(first_tables),))],
+        + [dma((len(first_tables),))]
+        + [
+            pltpu.VMEM(gains.shape, F32),
+            pltpu.VMEM(window.shape, F32),
+            pltpu.VMEM(phases.shape, F32),
+            pltpu.VMEM(coverage.shape, jnp.int32),
+            pltpu.VMEM(twist.shape, F32),
+            dma((5,)),
+        ],
         compiler_params=pltpu.CompilerParams(
             collective_id=0, has_side_effects=True, vmem_limit_bytes=55 * 1024 * 1024
         ),

time: 17.5 us -> 17.6 us (level)
  no operation moved by 1% of the time
where the time goes in v8:
time: 17.6 us; the launch traced here: 17.4 us
  Pallas kernels  17.2 us (98%)
    pallas_call x1, Pallas kernels, on_device(): pl.pallas_call(functools.partial(kernel, (facet_count, sub_count, pair_co...  14.6 us
    pallas_call x1, Pallas kernels, on_device(): pl.pallas_call(inverse_kernel, out_shape=jax.ShapeDtypeStruct((rows, 2 *...  2.65 us

profile of v8, /device:TPU:0, one launch (start us, length us, event | category | flops | bytes accessed | tf_op | source)
XLA Modules:
  0.0 17.4 jit_solution(16684257896125261621)
XLA Ops:
  0.0 0.0 copy-start
  0.0 0.0 copy-start.1
  0.0 0.0 copy-start.2
  0.0 0.0 copy-start.3
  0.0 0.0 copy-start.5
  0.0 0.0 copy-start.6
  0.0 0.0 copy-start.4
  0.0 14.6 %shard_map.127.returned = f32[2,4,16,256]{3,2,1,0:T(8,128)S(1)} custom-call(s32[8]{0:T(128)} %offsets_ref.3, f32[128,64,128]{2,1,0:T(8,128)} %bitcast.16, f32[32,128]{1,0:T(8,128)} %bitcast.12, f32[1,128]{1,0:T(1,128)} %bitcast.14, f32[2,512]{1,0:T(2,128)} %phases_far.1, s32[2,2,512]{2,1,0:T(2,128)} %coverage_far.1, f32[2,4,128]{2,1,0:T(4,128)} %constant.14.clone.twist_far, ...), custom_call_target="tpu_custom_call" | custom-call | tf_op jit(solution)/shard_map/pallas_call | solution.py:606
  14.6 0.0 copy-done
  14.6 0.0 copy-done.1
  14.7 0.0 copy-done.2
  14.7 0.0 copy-done.3
  14.7 0.0 copy-done.5
  14.7 0.0 copy-done.6
  14.7 0.0 copy-done.4
  14.7 2.6 %shard_map.128 = f32[16,64,128]{2,1,0:T(8,128)} custom-call(s32[8]{0:T(128)S(1)} %copy-done.5, f32[2,4,16,256]{3,2,1,0:T(8,128)S(1)} %shard_map.127.returned, f32[32,128]{1,0:T(8,128)S(1)} %bitcast.13, f32[1,128]{1,0:T(1,128)S(1)} %bitcast.15, f32[256,256]{1,0:T(8,128)S(1)} %copy-done, f32[32,8,256]{2,1,0:T(8,128)S(1)} %copy-done.1, ...), custom_call_target="tpu_custom_call" | custom-call | tf_op jit(solution)/shard_map/pallas_call | solution.py:647
Async XLA Ops:
  0.0 14.6 %copy-start = (f32[256,256]{1,0:T(8,128)S(1)}, f32[256,256]{1,0:T(8,128)}, u32[]{:S(2)}) copy-start(f32[256,256]{1,0:T(8,128)} %constant.19.clone.unit_t_far.unit_t_ref) | copy-start | bytes 786436
  0.0 14.6 %copy-start.1 = (f32[32,8,256]{2,1,0:T(8,128)S(1)}, f32[32,8,256]{2,1,0:T(8,128)}, u32[]{:S(2)}) copy-start(f32[32,8,256]{2,1,0:T(8,128)} %constant.17.clone.pick_far.pick_ref) | copy-start | bytes 786436
  0.0 14.6 %copy-start.2 = (f32[2,128,128]{2,1,0:T(8,128)S(1)}, f32[2,128,128]{2,1,0:T(8,128)}, u32[]{:S(2)}) copy-start(f32[2,128,128]{2,1,0:T(8,128)} %constant.16.clone.turn_far.turn_ref) | copy-start | bytes 393220
  0.0 14.7 %copy-start.3 = (f32[256,256]{1,0:T(8,128)S(1)}, f32[256,256]{1,0:T(8,128)}, u32[]{:S(2)}) copy-start(f32[256,256]{1,0:T(8,128)} %constant.20.clone.outer_t_ref) | copy-start | bytes 786436
  0.0 14.7 %copy-start.5 = (s32[8]{0:T(128)S(1)}, s32[8]{0:T(128)}, u32[]{:S(2)}) copy-start(s32[8]{0:T(128)} %offsets_ref.3) | copy-start | bytes 100
  0.0 14.7 %copy-start.6 = (f32[128]{0:T(128)S(1)}, f32[128]{0:T(128)}, u32[]{:S(2)}) copy-start(f32[128]{0:T(128)} %param.15) | copy-start | bytes 1540
  0.0 14.7 %copy-start.4 = (f32[1,4096]{1,0:T(1,128)S(1)}, f32[1,4096]{1,0:T(1,128)}, u32[]{:S(2)}) copy-start(f32[1,4096]{1,0:T(1,128)} %param.14) | copy-start | bytes 49156

commit v9 on v7

--- a/solution.py
+++ b/solution.py
@@ -162,13 +162,14 @@
     pick_far,
     unit_far,
     unit_t_far,
-    returned,
+    segments,
     image,
     gain,
     cut,
     sent,
     arrived,
     back,
+    returned,
     ordered,
     counts,
     expanded,
@@ -448,6 +449,7 @@
         for f in range(facet_count):
             back[h, f, :, :width] = sums[f][0]
             back[h, f, :, width:] = sums[f][1]
+        copies = []
         for i, mate in enumerate(far_first):
             copy = pltpu.make_async_remote_copy(
                 src_ref=back.at[h, mate],
@@ -458,61 +460,54 @@
                 device_id_type=MESH,
             )
             copy.start()
-            backward.append(copy)
+            copies.append(copy)
+        backward.append(copies)
         returned[h, facet] = back[h, facet]
-    for copy in backward:
-        copy.wait()
+    win_first = jnp.where(is_first, window_rows, 0.0)
+    win_second = jnp.where(is_first, 0.0, window_rows)
+    for h in range(halves):
+        for copy in backward[h]:
+            copy.wait()
+        rows_h = slice(h * part, (h + 1) * part)
+        tc, ts = turn_cos[rows_h], turn_sin[rows_h]
+        unturned = []
+        for g in range(facet_count):
+            real, imag = returned[h, g, :, :width], returned[h, g, :, width:]
+            unturned.append(
+                jnp.concatenate([real * tc - imag * ts, real * ts + imag * tc], axis=1)
+            )
+        mixed = mm(split(jnp.concatenate(unturned, axis=0)), unit_t)
+        for g in range(facet_count):
+            cols = slice(g * width, (g + 1) * width)
+            for c in range(2):
+                piece = mixed[g * part : (g + 1) * part, c * width : (c + 1) * width]
+                for band, win in enumerate((win_first, win_second)):
+                    masked = piece * win[rows_h]
+                    for s in range(part // quads):
+                        at = (4 * (h * (part // quads) + s) + 2 * band + c) * quads
+                        segments[at : at + quads, cols] = masked[s * quads : (s + 1) * quads]
 
 
 def inverse_kernel(
     offsets_ref,
-    returned,
+    segments,
     correction_ref,
-    window_ref,
-    unit_t_ref,
     pick_ref,
     turn_ref,
     outer_t_ref,
     out_ref,
     gain,
-    segments,
     image,
     out_sem,
 ):
-    halves, facet_count, part, double = returned.shape
-    span = halves * part
-    width = double // 2
-    subs = offsets_ref.shape[0]
+    width = correction_ref.shape[1]
+    facet_count = segments.shape[1] // width
     low = pick_ref.shape[0]
     quads = width // low
     gain[pl.ds(0, low, stride=2), :] = correction_ref[...]
     gain[pl.ds(1, low, stride=2), :] = correction_ref[...]
     gains = gain[...]
-    first_q, turn_cos, turn_sin, is_first, window_rows = offset_tables(
-        offsets_ref, window_ref, quads
-    )
-    unturned = []
-    for g in range(facet_count):
-        whole = jnp.concatenate([returned[h, g] for h in range(halves)], axis=0)
-        real, imag = whole[:, :width], whole[:, width:]
-        unturned.append(
-            jnp.concatenate(
-                [real * turn_cos - imag * turn_sin, real * turn_sin + imag * turn_cos], axis=1
-            )
-        )
-    unturned = jnp.concatenate(unturned, axis=0)
-    mixed = mm(split(unturned), split(unit_t_ref[...]))
-    win_first = jnp.where(is_first, window_rows, 0.0)
-    win_second = jnp.where(is_first, 0.0, window_rows)
-    for g in range(facet_count):
-        cols = slice(g * width, (g + 1) * width)
-        for c in range(2):
-            part = mixed[g * span : (g + 1) * span, c * width : (c + 1) * width]
-            for h, win in enumerate((win_first, win_second)):
-                masked = part * win
-                for s in range(subs):
-                    at = (4 * s + 2 * h + c) * quads
-                    segments[at : at + quads, cols] = masked[s * quads : (s + 1) * quads]
+    first_q = [offsets_ref[s] // width for s in range(offsets_ref.shape[0])]
     picked = gather_pick(first_q, pick_ref)
     table_cos, table_sin = turn_ref[0], turn_ref[1]
     outer_t = split(outer_t_ref[...])
@@ -581,9 +576,9 @@
     held = coverage.shape[0] * coverage.shape[1]
     window = window.reshape(1, width)
     first_tables = [outer, turn, pick, unit, unit_t]
-    returned = pl.pallas_call(
+    segments = pl.pallas_call(
         functools.partial(kernel, (facet_count, sub_count, pair_count)),
-        out_shape=pltpu.VMEM(block, F32),
+        out_shape=pltpu.VMEM((4 * span, total), F32),
         in_specs=[smem, far] + [vmem] * 5 + [far] * len(first_tables),
         out_specs=vmem,
         scratch_shapes=[
@@ -592,6 +587,7 @@
             pltpu.VMEM((facet_count // pair_size, pair_size, span, 2 * width), F32),
             pltpu.VMEM((facet_count // pair_size, pair_size, span, 2 * width), F32),
             pltpu.VMEM((facet_count, span, 2 * width), F32),
+            pltpu.VMEM(block, F32),
             pltpu.VMEM(block, F32),
             pltpu.VMEM((held, total), F32),
             pltpu.VMEM((sub_count, pair_count, held, total), F32),
@@ -613,20 +609,19 @@
             collective_id=0, has_side_effects=True, vmem_limit_bytes=55 * 1024 * 1024
         ),
     )(offsets, image, gains, window, phases, coverage, jnp.asarray(twist), *map(jnp.asarray, first_tables))
-    second_tables = [unit_t, pick, turn, outer_t]
+    second_tables = [pick, turn, outer_t]
     result = pl.pallas_call(
         inverse_kernel,
         out_shape=jax.ShapeDtypeStruct((rows, 2 * lines, width), F32),
-        in_specs=[smem] + [vmem] * (3 + len(second_tables)),
+        in_specs=[smem] + [vmem] * (2 + len(second_tables)),
         out_specs=far,
         scratch_shapes=[
             pltpu.VMEM((2 * lines, width), F32),
-            pltpu.VMEM((4 * span, total), F32),
             pltpu.VMEM((rows, 2 * lines, width), F32),
             dma((facet_count,)),
         ],
         compiler_params=pltpu.CompilerParams(vmem_limit_bytes=48 * 1024 * 1024),
-    )(offsets, returned, gains, window, *map(jnp.asarray, second_tables))
+    )(offsets, segments, gains, *map(jnp.asarray, second_tables))
     result = jnp.transpose(result.reshape(rows, lines, 2, width), (0, 2, 1, 3))
     return result.reshape(1, rows, 2, length)
 

time: 17.5 us -> 17.4 us (level)
    pallas_call x1, Pallas kernels: 14.5 us -> 14.7 us  [on_device(): pl.pallas_call(functools.partial(kernel, (facet_count, sub_count, pair_co...]
    pallas_call x1, Pallas kernels: 2.65 us -> 2.44 us  [on_device(): pl.pallas_call(inverse_kernel, out_shape=jax.ShapeDtypeStruct((rows, 2 *...]
where the time goes in v9:
time: 17.4 us; the launch traced here: 17.2 us
  Pallas kernels  17.2 us (99%)
    pallas_call x1, Pallas kernels, on_device(): pl.pallas_call(functools.partial(kernel, (facet_count, sub_count, pair_co...  14.7 us
    pallas_call x1, Pallas kernels, on_device(): pl.pallas_call(inverse_kernel, out_shape=jax.ShapeDtypeStruct((rows, 2 *...  2.44 us

profile of v9, /device:TPU:0, one launch (start us, length us, event | category | flops | bytes accessed | tf_op | source)
XLA Modules:
  0.0 17.2 jit_solution(5696346108798402014)
XLA Ops:
  0.0 0.0 copy-start
  0.0 0.0 copy-start.1
  0.0 0.0 copy-start.2
  0.0 0.0 copy-start.4
  0.0 0.0 copy-start.3
  0.0 14.7 %shard_map.127.segments = f32[128,512]{1,0:T(8,128)S(1)} custom-call(s32[8]{0:T(128)} %offsets_ref.3, f32[128,64,128]{2,1,0:T(8,128)} %bitcast.14, f32[32,128]{1,0:T(8,128)} %bitcast.12, f32[1,128]{1,0:T(1,128)} %bitcast.15, f32[2,512]{1,0:T(2,128)} %phases_ref.1, s32[2,2,512]{2,1,0:T(2,128)} %coverage_ref.1, f32[2,4,128]{2,1,0:T(4,128)} %constant.14.clone.twist_ref, ...), custom_call_target="tpu_custom_call" | custom-call | tf_op jit(solution)/shard_map/pallas_call | solution.py:579
  14.8 0.0 copy-done
  14.8 0.0 copy-done.1
  14.8 0.0 copy-done.2
  14.8 0.0 copy-done.4
  14.8 0.0 copy-done.3
  14.8 2.4 %shard_map.128 = f32[16,64,128]{2,1,0:T(8,128)} custom-call(s32[8]{0:T(128)S(1)} %copy-done.4, f32[128,512]{1,0:T(8,128)S(1)} %shard_map.127.segments, f32[32,128]{1,0:T(8,128)S(1)} %bitcast.13, f32[32,8,256]{2,1,0:T(8,128)S(1)} %copy-done, f32[2,128,128]{2,1,0:T(8,128)S(1)} %copy-done.1, f32[256,256]{1,0:T(8,128)S(1)} %copy-done.2), custom_call_target="tpu_custom_call" | custom-call | tf_op jit(solution)/shard_map/pallas_call | solution.py:613
Async XLA Ops:
  0.0 14.8 %copy-start = (f32[32,8,256]{2,1,0:T(8,128)S(1)}, f32[32,8,256]{2,1,0:T(8,128)}, u32[]{:S(2)}) copy-start(f32[32,8,256]{2,1,0:T(8,128)} %constant.17.clone.pick_far.pick_ref) | copy-start | bytes 786436
  0.0 14.8 %copy-start.1 = (f32[2,128,128]{2,1,0:T(8,128)S(1)}, f32[2,128,128]{2,1,0:T(8,128)}, u32[]{:S(2)}) copy-start(f32[2,128,128]{2,1,0:T(8,128)} %constant.16.clone.turn_far.turn_ref) | copy-start | bytes 393220
  0.0 14.8 %copy-start.2 = (f32[256,256]{1,0:T(8,128)S(1)}, f32[256,256]{1,0:T(8,128)}, u32[]{:S(2)}) copy-start(f32[256,256]{1,0:T(8,128)} %constant.20.clone.outer_t_ref) | copy-start | bytes 786436
  0.0 14.8 %copy-start.4 = (s32[8]{0:T(128)S(1)}, s32[8]{0:T(128)}, u32[]{:S(2)}) copy-start(s32[8]{0:T(128)} %offsets_ref.3) | copy-start | bytes 100
  0.0 14.8 %copy-start.3 = (f32[1,4096]{1,0:T(1,128)S(1)}, f32[1,4096]{1,0:T(1,128)}, u32[]{:S(2)}) copy-start(f32[1,4096]{1,0:T(1,128)} %param.14) | copy-start | bytes 49156
